TPU v7x, 128 devices: a whole 4x4x4 slice. The times are simulated.
128 devices in a mesh: feat: 8 (over x, core), rows: 16 (over z, y).
Axes of the slice: x: 4, y: 4, z: 4, core: 2. Of those that a mesh axis runs over, the one named last changes fastest.
Arguments:
- features: bfloat16 [128, 128, 768], P('feat', None, 'rows'), may hold values from -6 to 6
- w_in: bfloat16 [128, 256], replicated, may hold values from -0.5 to 0.5
- bias: float32 [256], replicated, may hold values from -4 to 4
- tiles: bfloat16 [768, 8, 128, 128], P(('feat', 'rows')), may hold values from 0 to 1, as said below
- tile_cols: int32 [768, 8], P(('feat', 'rows')), may hold values from 0 to 767, as said below
- tile_counts: int32 [768], P(('feat', 'rows')), may hold values from 1 to 8, as said below
- cotangent: bfloat16 [98304, 256], P(('feat', 'rows')), may hold values from -6 to 6
Outputs:
- hidden: bfloat16 [98304, 256], P(('feat', 'rows'))
- weight_grad: float32 [128, 256], P('feat')
Inputs may be any that keep to these rules, and one draw needn't show every extreme that they name: Each block row's count lies between 1 and 8; in every draw some device owns a block row with 8 live slots. Slots k >= tile_counts[I] are ignored. `tile_cols`: block row I on the device owning blocks s * 6 to s * 6 + 6 - 1 (s = I // 6) names column blocks J with J // 96 = I // 96 and (J - (s % 16) * 6 + 2) mod 96 below 10: its own blocks or up to 2 blocks of the neighbouring devices in its cycle, wrapping; both ends are reached. `tiles`: entries are 0 or 1.
All inputs are finite; a program needn't handle non-finite values.
Results may differ from a plain program's by a relative error of at most 0.008.
Values may be sent and summed in bfloat16 or wider, within the bound.
No kernel may reach another device: no remote copies, remote signals or barrier semaphores. Data moves between devices by JAX's collectives and lax.ppermute only.
A program may use at most 64 MiB of HBM per device.

v0:
```python
import jax
import jax.numpy as jnp
from jax import lax
from jax.sharding import PartitionSpec as P

HALO_BLK = 2


def padded(cells, sides, width):
    for axis, dim in sides:
        count = lax.axis_size(axis)
        head = lax.slice_in_dim(cells, 0, width, axis=dim)
        tail = lax.slice_in_dim(cells, cells.shape[dim] - width, cells.shape[dim], axis=dim)
        cells = jnp.concatenate(
            [
                lax.ppermute(tail, axis, [(i, (i + 1) % count) for i in range(count)]),
                cells,
                lax.ppermute(head, axis, [((i + 1) % count, i) for i in range(count)]),
            ],
            axis=dim,
        )
    return cells


def shifted(block, axis, distance):
    devices = range(lax.axis_size(axis))
    route = [((i - distance) % len(devices), i) for i in devices]
    return lax.ppermute(block, axis, route)


def gelu_parts(values):
    inner = 0.7978845608 * (values + 0.044715 * values * values * values)
    tangent = jnp.tanh(inner)
    output = 0.5 * values * (1.0 + tangent)
    slope = 0.5 * (1.0 + tangent) + 0.5 * values * (1.0 - tangent * tangent) * 0.7978845608 * (
        1.0 + 3.0 * 0.044715 * values * values
    )
    return (output, slope)


def halo_projected(projected, margin):
    return padded(projected, (("rows", 0),), margin)


def body(features, w_in, bias, tiles, tile_cols, tile_counts, cotangent):
    block_rows, slot_count, tile_side, unused_side = tiles.shape
    hidden_width = w_in.shape[1]
    feat_size = lax.axis_size("feat")
    row_size = lax.axis_size("rows")
    slice_width = w_in.shape[0] // feat_size
    nodes_dev = block_rows * tile_side
    sub_rows = nodes_dev // row_size
    feat_id = lax.axis_index("feat")
    row_id = lax.axis_index("rows")
    margin = HALO_BLK * tile_side
    w_own = lax.dynamic_slice_in_dim(w_in, feat_id * slice_width, slice_width, 0)
    partial_value = jnp.einsum(
        "cdn,ch->dnh", features, w_own, preferred_element_type=jnp.float32
    ).astype(jnp.bfloat16)
    received = lax.all_to_all(
        partial_value, ("feat", "rows"), split_axis=0, concat_axis=0, tiled=True
    )
    received = received.reshape(feat_size, nodes_dev, hidden_width)
    projected = jnp.sum(received.astype(jnp.float32), axis=0).astype(jnp.bfloat16)
    extended = halo_projected(projected, margin)
    ext_count = block_rows + 2 * HALO_BLK
    ext_blocks = extended.reshape(ext_count, tile_side, hidden_width)
    cycle_size = block_rows * row_size
    local_cols = (tile_cols - feat_id * cycle_size - row_id * block_rows + HALO_BLK) % cycle_size
    slot_ids = jnp.arange(slot_count, dtype=jnp.int32)
    live_slot = (slot_ids[None, :] < tile_counts[:, None]).astype(jnp.bfloat16)
    masked = tiles * live_slot[:, :, None, None]
    degree = jnp.sum(masked, axis=(1, 3), dtype=jnp.float32)
    neighbours = ext_blocks[local_cols]
    summed_rows = jnp.einsum(
        "bkij,bkjh->bih", masked, neighbours, preferred_element_type=jnp.float32
    )
    own_rows = projected.reshape(block_rows, tile_side, hidden_width).astype(jnp.float32)
    pre_act = (own_rows + summed_rows) / (degree[:, :, None] + 1.0) + bias
    activated, slope = gelu_parts(pre_act)
    hidden = activated.astype(jnp.bfloat16).reshape(nodes_dev, hidden_width)
    scaled = (
        cotangent.reshape(block_rows, tile_side, hidden_width).astype(jnp.float32)
        * slope
        / (degree[:, :, None] + 1.0)
    ).astype(jnp.bfloat16)
    targets = jnp.arange(ext_count, dtype=jnp.int32)
    onehot = (local_cols[:, :, None] == targets[None, None, :]).astype(jnp.bfloat16)
    combined = jnp.einsum(
        "bkq,bkij->qbij", onehot, masked, preferred_element_type=jnp.float32
    ).astype(jnp.bfloat16)
    ext_sums = jnp.einsum("qbij,bih->qjh", combined, scaled, preferred_element_type=jnp.float32)
    from_before = shifted(ext_sums[block_rows + HALO_BLK :].astype(jnp.bfloat16), "rows", 1).astype(
        jnp.float32
    )
    from_after = shifted(ext_sums[:HALO_BLK].astype(jnp.bfloat16), "rows", -1).astype(jnp.float32)
    own_sums = ext_sums[HALO_BLK : HALO_BLK + block_rows] + scaled.astype(jnp.float32)
    own_sums = own_sums.at[:HALO_BLK].add(from_before)
    own_sums = own_sums.at[block_rows - HALO_BLK :].add(from_after)
    grad_proj = own_sums.astype(jnp.bfloat16).reshape(nodes_dev, hidden_width)
    pieces = lax.all_to_all(
        grad_proj.reshape(row_size, sub_rows, hidden_width),
        "rows",
        split_axis=0,
        concat_axis=0,
        tiled=True,
    )
    grad_slice = jnp.einsum(
        "cdn,dnh->ch",
        features,
        lax.all_gather(pieces, "feat", axis=0, tiled=True),
        preferred_element_type=jnp.float32,
    )
    weight_grad = lax.psum(grad_slice, "rows")
    return (hidden, weight_grad)


def solution(mesh):
    in_specs = (
        P("feat", None, "rows"),
        P(),
        P(),
        P(("feat", "rows"), None, None, None),
        P(("feat", "rows"), None),
        P(("feat", "rows")),
        P(("feat", "rows"), None),
    )
    out_specs = (P(("feat", "rows"), None), P("feat", None))
    return jax.shard_map(body, mesh=mesh, in_specs=in_specs, out_specs=out_specs, check_vma=False)
```

profile of v0, /device:TPU:0, one launch (start us, length us, event | category | flops | bytes accessed | tf_op | source)
XLA Modules:
  0.0 216.6 jit_solution(2524314712389904341)
XLA Ops:
  7.2 0.0 copy-start
  7.2 0.8 copy-done
  8.0 1.9 convert_bitcast_fusion.1
  9.9 3.2 %copy.17 = bf16[128,48,256]{2,1,0:T(8,128)(2,1)} copy(bf16[128,48,256]{0,2,1:T(8,128)(2,1)S(1)} %convert_bitcast_fusion.1) | data formatting | bytes 6291456 | tf_op jit(solution)/shard_map/convert_element_type | solution.py:59
  13.1 0.0 copy-start.9
  13.1 0.0 copy-start.8
  13.1 11.1 %all-to-all-start = ((bf16[128,48,256]{2,1,0:T(8,128)(2,1)}), bf16[128,48,256]{2,1,0:T(8,128)(2,1)S(1)}, u32[]{:S(2)}, u32[]{:S(2)}) async-start(bf16[128,48,256]{2,1,0:T(8,128)(2,1)} %copy.17), calls=%async_computation | async-start | bytes 6291456 | tf_op jit(solution)/shard_map/all_to_all | solution.py:60
  24.3 0.0 all-gather.2.cloned.1.call-start
  24.3 0.0 copy-done.9
  24.3 0.1 fusion.27
  24.4 0.0 copy-done.8
  24.4 2.0 convert_reduce_fusion
  26.5 0.0 copy-start.1
  26.5 1.1 copy-done.1
  27.6 3.1 %convert_bitcast_fusion = bf16[10,6,128,128]{3,0,2,1:T(8,128)(2,1)} fusion(bf16[6,8,128,128]{3,2,1,0:T(8,128)(2,1)S(1)} %get-tuple-element.27, s32[6,8]{1,0:T(8,128)S(1)} %get-tuple-element.29), kind=kOutput, calls=%fused_computation.2 | convolution fusion | flops 16712160 | bytes 3539136 | tf_op jit(solution)/shard_map/bkq,bkij->qbij/dot_general | solution.py:89
  30.7 33.8 %all-to-all-done = bf16[128,48,256]{2,1,0:T(8,128)(2,1)S(1)} async-done(((bf16[128,48,256]{2,1,0:T(8,128)(2,1)}), bf16[128,48,256]{2,1,0:T(8,128)(2,1)S(1)}, u32[]{:S(2)}, u32[]{:S(2)}) %all-to-all-start) | async-done | bytes 3145760 | tf_op jit(solution)/shard_map/all_to_all | solution.py:60
  64.5 0.4 bitcast_reduce_fusion
  64.9 0.0 copy-start.4
  65.0 0.7 copy-done.4
  65.7 0.7 collective-permute-start
  66.4 4.7 %collective-permute-start.1 = (bf16[256,256]{1,0:T(8,128)(2,1)S(1)}, bf16[256,256]{1,0:T(8,128)(2,1)S(1)}, u32[]{:S(2)}, u32[]{:S(2)}) collective-permute-start(bf16[256,256]{1,0:T(8,128)(2,1)S(1)} %get-tuple-element.35), channel_id=1, source_target_pairs={{1,0},{2,1},{3,2},{4,3},{5,4},{6,5},{7,6},{8,7},{9,8},{10,9},{11,1... | collective-permute-start | bytes 393224 | tf_op jit(solution)/shard_map/ppermute | solution.py:18
  71.1 0.1 reshape.114
  71.2 2.9 %collective-permute-done = bf16[256,256]{1,0:T(8,128)(2,1)S(1)} collective-permute-done((bf16[256,256]{1,0:T(8,128)(2,1)S(1)}, bf16[256,256]{1,0:T(8,128)(2,1)S(1)}, u32[]{:S(2)}, u32[]{:S(2)}) %collective-permute-start) | collective-permute-done | bytes 131104 | tf_op jit(solution)/shard_map/ppermute | solution.py:16
  74.1 0.0 collective-permute-done.1
  74.1 1.0 pad_maximum_fusion
  75.1 0.0 copy-start.2
  75.1 0.0 copy-start.5
  75.1 0.0 copy-start.10
  75.2 2.5 %gather_fusion = bf16[48,128,256]{2,1,0:T(8,128)(2,1)} fusion(bf16[10,128,256]{2,1,0:T(8,128)(2,1)S(1)} %bitcast.47, s32[1024]{0:T(1024)S(1)} %pad_clamp_fusion), kind=kCustom, calls=%fused_computation | custom fusion | bytes 6291648 | tf_op jit(solution)/shard_map/gather | solution.py:74
  77.7 0.0 copy-done.2
  77.7 0.0 copy-done.5
  77.7 0.0 copy-done.10
  77.7 0.0 copy-start.3
  77.7 0.0 copy-start.7
  77.7 2.8 %fusion.8 = f32[6,128,256]{2,1,0:T(8,128)S(1)} fusion(bf16[6,8,128,128]{3,2,1,0:T(8,128)(2,1)S(1)} %copy-done.2, bf16[6,8,128,256]{3,2,1,0:T(8,128)(2,1)} %bitcast.49, bf16[6,128,256]{2,1,0:T(8,128)(2,1)S(1)} %bitcast.50, f32[256]{0:T(256)S(1)} %copy-done.10, f32[6,128]{1,0:T(8,128)S(1)} %broadcast_add_fusion), kind=kOutput, calls=%fused_computation.12 | convolution fusion | flops 403439616 | bytes 5902336 | tf_op jit(solution)/shard_map/bkij,bkjh->bih/dot_general | solution.py:75
  80.5 0.0 copy-done.3
  80.5 0.1 copy-done.7
  80.6 1.5 fusion.32
  82.1 0.1 collective-permute-start.2
  82.2 0.0 copy-start.6
  82.2 1.4 slice_add_fusion
  83.6 5.3 %collective-permute-start.3 = (bf16[2,128,256]{2,1,0:T(8,128)(2,1)S(1)}, bf16[2,128,256]{2,1,0:T(8,128)(2,1)S(1)}, u32[]{:S(2)}, u32[]{:S(2)}) collective-permute-start(bf16[2,128,256]{2,1,0:T(8,128)(2,1)S(1)} %get-tuple-element.32), channel_id=1, source_target_pairs={{1,0},{2,1},{3,2},{4,3},{5,4},{6,5},{7,6},{8,7},{9,8},{10,9},{11,1... | collective-permute-start | bytes 393224 | tf_op jit(solution)/shard_map/ppermute | solution.py:28
  88.9 1.6 collective-permute-done.2
  90.5 0.1 fusion.19
  90.5 0.9 collective-permute-done.3
  91.4 0.1 fusion.18
  91.5 16.3 %all_to_all.10 = bf16[16,48,256]{2,1,0:T(8,128)(2,1)S(1)} all-to-all(bf16[16,48,256]{2,1,0:T(8,128)(2,1)S(1)} %bitcast.51), channel_id=1, replica_groups=mesh['feat'=8,'rows'=16] {'rows'}, dimensions={0} | all-to-all | bytes 786432 | tf_op jit(solution)/shard_map/all_to_all | solution.py:101
  107.9 0.9 copy.20
  108.8 0.0 all-gather.2.cloned.1.call-update
  108.8 24.0 %all-gather.2.cloned.1.call-done = bf16[128,48,256]{2,0,1:T(8,128)(2,1)} async-done(((bf16[16,48,256]{2,0,1:T(8,128)(2,1)}), bf16[128,48,256]{2,0,1:T(8,128)(2,1)}) %all-gather.2.cloned.1.call-update) | async-done | bytes 3145744 | tf_op jit(solution)/shard_map/all_gather | solution.py:111
  132.8 0.0 copy-done.6
  132.8 2.4 %convolution_bitcast_fusion.1 = f32[16,256]{1,0:T(8,128)S(1)} fusion(bf16[128,48,256]{2,0,1:T(8,128)(2,1)} %all-gather.2.cloned.1.call-done, bf16[16,128,48]{1,2,0:T(8,128)(2,1)S(1)} %copy-done.6), kind=kOutput, calls=%fused_computation.15 | convolution fusion | flops 50331648 | bytes 3358720 | tf_op jit(solution)/shard_map/cdn,dnh->ch/dot_general | solution.py:108
  135.2 74.5 %psum.7 = f32[16,256]{1,0:T(8,128)} all-reduce(f32[16,256]{1,0:T(8,128)S(1)} %convolution_bitcast_fusion.1), channel_id=1, replica_groups=mesh['feat'=8,'rows'=16] {'rows'}, use_global_device_ids=true, to_apply=%region_2.3 | all-reduce | flops 4096 | bytes 32768 | tf_op jit(solution)/shard_map/psum | solution.py:114
  (6 shorter events, 0.1 us)
Async XLA Ops:
  7.2 0.8 copy-start
  13.1 11.2 %copy-start.9 = (s32[6]{0:T(128)S(1)}, s32[6]{0:T(128)}, u32[]{:S(2)}) copy-start(s32[6]{0:T(128)} %param.16) | copy-start | bytes 76
  13.1 11.3 %copy-start.8 = (s32[6,8]{1,0:T(8,128)S(1)}, s32[6,8]{1,0:T(8,128)}, u32[]{:S(2)}) copy-start(s32[6,8]{1,0:T(8,128)} %param.15) | copy-start | bytes 580
  13.1 51.4 %all-to-all-start = ((bf16[128,48,256]{2,1,0:T(8,128)(2,1)}), bf16[128,48,256]{2,1,0:T(8,128)(2,1)S(1)}, u32[]{:S(2)}, u32[]{:S(2)}) async-start(bf16[128,48,256]{2,1,0:T(8,128)(2,1)} %copy.17), calls=%async_computation | async-start | bytes 6291456 | tf_op jit(solution)/shard_map/all_to_all | solution.py:60
  24.3 108.5 %all-gather.2.cloned.1.call-start = ((), (), s32[]{:S(2)}) async-start(), calls=%async_computation.2 | async-start | bytes 3538944 | tf_op jit(solution)/shard_map/all_gather | solution.py:111
  26.5 1.1 copy-start.1
  64.9 0.7 copy-start.4
  65.7 8.4 %collective-permute-start = (bf16[256,256]{1,0:T(8,128)(2,1)S(1)}, bf16[256,256]{1,0:T(8,128)(2,1)S(1)}, u32[]{:S(2)}, u32[]{:S(2)}) collective-permute-start(bf16[256,256]{1,0:T(8,128)(2,1)S(1)} %get-tuple-element.34), channel_id=1, source_target_pairs={{0,1},{1,2},{2,3},{3,4},{4,5},{5,6},{6,7},{7,8},{8,9},{9,10},{10,1... | collective-permute-start | bytes 393224 | tf_op jit(solution)/shard_map/ppermute | solution.py:16
  66.4 7.7 %collective-permute-start.1 = (bf16[256,256]{1,0:T(8,128)(2,1)S(1)}, bf16[256,256]{1,0:T(8,128)(2,1)S(1)}, u32[]{:S(2)}, u32[]{:S(2)}) collective-permute-start(bf16[256,256]{1,0:T(8,128)(2,1)S(1)} %get-tuple-element.35), channel_id=1, source_target_pairs={{1,0},{2,1},{3,2},{4,3},{5,4},{6,5},{7,6},{8,7},{9,8},{10,9},{11,1... | collective-permute-start | bytes 393224 | tf_op jit(solution)/shard_map/ppermute | solution.py:18
  75.1 2.6 %copy-start.2 = (bf16[6,8,128,128]{3,2,1,0:T(8,128)(2,1)S(1)}, bf16[6,8,128,128]{3,2,1,0:T(8,128)(2,1)}, u32[]{:S(2)}) copy-start(bf16[6,8,128,128]{3,2,1,0:T(8,128)(2,1)} %copy-done.1) | copy-start | bytes 4718596
  75.1 2.6 %copy-start.5 = (bf16[768,256]{1,0:T(8,128)(2,1)S(1)}, bf16[768,256]{1,0:T(8,128)(2,1)}, u32[]{:S(2)}) copy-start(bf16[768,256]{1,0:T(8,128)(2,1)} %copy-done.4) | copy-start | bytes 1179652
  75.1 2.6 %copy-start.10 = (f32[256]{0:T(256)S(1)}, f32[256]{0:T(256)}, u32[]{:S(2)}) copy-start(f32[256]{0:T(256)} %param.13) | copy-start | bytes 3076
  77.7 2.8 %copy-start.3 = (bf16[10,6,128,128]{3,0,2,1:T(8,128)(2,1)S(1)}, bf16[10,6,128,128]{3,0,2,1:T(8,128)(2,1)}, u32[]{:S(2)}) copy-start(bf16[10,6,128,128]{3,0,2,1:T(8,128)(2,1)} %convert_bitcast_fusion) | copy-start | bytes 5898244
  77.7 2.9 %copy-start.7 = (bf16[768,256]{1,0:T(8,128)(2,1)S(1)}, bf16[768,256]{1,0:T(8,128)(2,1)}, u32[]{:S(2)}) copy-start(bf16[768,256]{1,0:T(8,128)(2,1)} %param.17) | copy-start | bytes 1179652
  82.1 8.4 %collective-permute-start.2 = (bf16[2,128,256]{2,1,0:T(8,128)(2,1)S(1)}, bf16[2,128,256]{2,1,0:T(8,128)(2,1)S(1)}, u32[]{:S(2)}, u32[]{:S(2)}) collective-permute-start(bf16[2,128,256]{2,1,0:T(8,128)(2,1)S(1)} %get-tuple-element.33), channel_id=1, source_target_pairs={{15,0},{0,1},{1,2},{2,3},{3,4},{4,5},{5,6},{6,7},{7,8},{8,9},{9,10... | collective-permute-start | bytes 393224 | tf_op jit(solution)/shard_map/ppermute | solution.py:28
  82.2 50.6 %copy-start.6 = (bf16[16,128,48]{1,2,0:T(8,128)(2,1)S(1)}, bf16[16,128,48]{1,2,0:T(8,128)(2,1)}, u32[]{:S(2)}) copy-start(bf16[16,128,48]{1,2,0:T(8,128)(2,1)} %param.11) | copy-start | bytes 589828
  83.6 7.9 %collective-permute-start.3 = (bf16[2,128,256]{2,1,0:T(8,128)(2,1)S(1)}, bf16[2,128,256]{2,1,0:T(8,128)(2,1)S(1)}, u32[]{:S(2)}, u32[]{:S(2)}) collective-permute-start(bf16[2,128,256]{2,1,0:T(8,128)(2,1)S(1)} %get-tuple-element.32), channel_id=1, source_target_pairs={{1,0},{2,1},{3,2},{4,3},{5,4},{6,5},{7,6},{8,7},{9,8},{10,9},{11,1... | collective-permute-start | bytes 393224 | tf_op jit(solution)/shard_map/ppermute | solution.py:28
Sparse Core Ops, SparseCore 0:
  108.9 23.8 all-gather.1
where the time goes:
time: 217 us
  blocking collectives  90.9 us (42%)
  waiting for transfers between devices  63.2 us (29%)
  starting transfers between devices  22 us (10%)
  between operations  14.2 us (7%)
  matrix products  11.6 us (5%)
  local copies, waits for them, and re-layouts  9.55 us (4%)
  other arithmetic  5.11 us (2%)
    psum x1, blocking collectives, body(): weight_grad = lax.psum(grad_slice, 'rows')  74.5 us
    all_to_all x1, waiting for transfers between devices, body(): lax.all_to_all(partial_value, ('feat', 'rows'), split_axis=0, concat_axis...  33.8 us
    all_gather x1, waiting for transfers between devices, body(): lax.all_gather(pieces, 'feat', axis=0, tiled=True)  24 us
    all_to_all x1, blocking collectives, body(): lax.all_to_all(grad_proj.reshape(row_size, sub_rows, hidden_width), 'rows...  16.3 us
    all_to_all x1, starting transfers between devices, body(): lax.all_to_all(partial_value, ('feat', 'rows'), split_axis=0, concat_axis...  11.1 us
    ppermute x2, starting transfers between devices, shifted(): return lax.ppermute(block, axis, route)  5.42 us
    ppermute x1, starting transfers between devices, padded(): lax.ppermute(head, axis, [((i + 1) % count, i) for i in range(count)])  4.74 us
  transfers between devices with their start and end apart: 6, of which 5 were waited for; matrix products, arithmetic and copies ran while one was open for 3% of the time, Pallas kernels for 0%

commit v1 on v0

v1 whole, which is shorter than its diff:
```python
import jax
import jax.numpy as jnp
from jax import lax
from jax.experimental import pallas as pl
from jax.experimental.pallas import tpu as pltpu
from jax.sharding import PartitionSpec as P

HALO_BLK = 2
F32 = jnp.float32
BF16 = jnp.bfloat16


def adjacency_kernel(cols_ref, counts_ref, base_ref, tiles_ref, adj_ref, *, rows_axis, cycle):
    nb, slots, side, _ = tiles_ref.shape
    adj_ref[...] = jnp.zeros_like(adj_ref)
    eye = (
        lax.broadcasted_iota(jnp.int32, (side, side), 0)
        == lax.broadcasted_iota(jnp.int32, (side, side), 1)
    )
    eye = jnp.where(eye, 1.0, 0.0).astype(BF16)
    base = base_ref[0]
    for b in range(nb):
        rows = pl.ds(b * side, side)
        adj_ref[rows, pl.ds((b + HALO_BLK) * side, side)] = eye
        for k in range(slots):

            @pl.when(k < counts_ref[b])
            def _():
                block = lax.rem(cols_ref[b, k] - base + HALO_BLK + cycle, cycle)
                at = (rows, pl.ds(pl.multiple_of(block * side, side), side))
                adj_ref[at] = adj_ref[at] + tiles_ref[b, k]


def layer_kernel(recv_ref, adj_ref, w_ref, bias_ref, cot_ref, hidden_ref, grad_ref, x_ref):
    groups, senders, width, lanes = recv_ref.shape
    features = groups * width
    nodes = hidden_ref.shape[0]
    ext = x_ref.shape[0]
    halo = (ext - nodes) // 2
    part = nodes // senders
    x_ref[:, features:] = jnp.ones((ext, features), BF16)
    for r in range(senders):
        piece = recv_ref[:, r].reshape(features, lanes)
        piece = jnp.concatenate([piece, jnp.zeros((features, 128 - lanes), BF16)], axis=1).T
        x_ref[halo + r * part : halo + (r + 1) * part, :features] = piece[:part]
        first, last = r * part, (r + 1) * part
        if first < halo:
            n = min(last, halo) - first
            x_ref[halo + nodes + first : halo + nodes + first + n, :features] = piece[part : part + n]
        if last > nodes - halo:
            skip = max(nodes - halo - first, 0)
            to = first + skip - (nodes - halo)
            x_ref[to : to + part - skip, :features] = piece[part + skip : 2 * part]
    w = w_ref[...]
    ww = jnp.concatenate([w, w], axis=0)
    bias = bias_ref[...]
    side = 128
    hidden_width = w.shape[1]
    total = jnp.zeros((2 * features, hidden_width), F32)
    for b in range(nodes // side):
        rows = pl.ds(b * side, side)
        both = jnp.dot(adj_ref[rows, :], x_ref[...], preferred_element_type=F32)
        y = both[:, :features]
        inv = 1.0 / both[:, features:]
        inv = jnp.concatenate([inv] * (hidden_width // features), axis=1)
        y_hi = y.astype(BF16)
        y_lo = (y - y_hi.astype(F32)).astype(BF16)
        yy = jnp.concatenate([y_hi, y_lo], axis=1)
        v = jnp.dot(yy, ww, preferred_element_type=F32) * inv + bias
        v2 = v * v
        t = jnp.tanh(0.7978845608 * (v + 0.044715 * v2 * v))
        half = 0.5 * (1.0 + t)
        hidden_ref[rows, :] = (v * half).astype(BF16)
        slope = half + 0.5 * v * (1.0 - t * t) * 0.7978845608 * (1.0 + 3.0 * 0.044715 * v2)
        scaled = (cot_ref[rows, :].astype(F32) * slope * inv).astype(BF16)
        total += lax.dot_general(yy, scaled, (((0,), (0,)), ((), ())), preferred_element_type=F32)
    grad_ref[...] = total[:features] + total[features:]


def body(features, w_in, bias, tiles, tile_cols, tile_counts, cotangent):
    block_rows, slots, side, _ = tiles.shape
    n_features, hidden_width = w_in.shape
    feat_size = lax.axis_size("feat")
    row_size = lax.axis_size("rows")
    nodes = block_rows * side
    halo = HALO_BLK * side
    width, owners, part = features.shape
    feat_id = lax.axis_index("feat")
    row_id = lax.axis_index("rows")
    cycle = block_rows * row_size

    by_owner = features.transpose(1, 0, 2)
    ring = by_owner.reshape(feat_size, row_size, width, part)
    beside = jnp.where(row_id * 2 < row_size, jnp.roll(ring, -1, axis=1), jnp.roll(ring, 1, axis=1))
    send = jnp.concatenate([by_owner, beside.reshape(by_owner.shape)], axis=2)
    recv = lax.all_to_all(send, ("feat", "rows"), split_axis=0, concat_axis=0, tiled=True)
    recv = recv.reshape(feat_size, row_size, width, 2 * part)

    base = (feat_id * cycle + row_id * block_rows).reshape(1).astype(jnp.int32)
    ext = nodes + 2 * halo
    vmem = pl.BlockSpec(memory_space=pltpu.VMEM)
    smem = pl.BlockSpec(memory_space=pltpu.SMEM)
    adj = pl.pallas_call(
        lambda *refs: adjacency_kernel(*refs, rows_axis="rows", cycle=cycle),
        out_shape=jax.ShapeDtypeStruct((nodes, ext), BF16),
        in_specs=[smem, smem, smem, vmem],
        out_specs=vmem,
        compiler_params=pltpu.CompilerParams(vmem_limit_bytes=16 * 2**20),
        cost_estimate=pl.CostEstimate(flops=2 * 10**6, bytes_accessed=4 * 10**6, transcendentals=0),
        name="adjacency",
    )(tile_cols, tile_counts, base, tiles)
    hidden, terms = pl.pallas_call(
        layer_kernel,
        out_shape=(
            jax.ShapeDtypeStruct((nodes, hidden_width), BF16),
            jax.ShapeDtypeStruct((n_features, hidden_width), F32),
        ),
        in_specs=[vmem] * 5,
        out_specs=(vmem, vmem),
        scratch_shapes=[pltpu.VMEM((ext, 2 * n_features), BF16)],
        compiler_params=pltpu.CompilerParams(vmem_limit_bytes=24 * 2**20),
        cost_estimate=pl.CostEstimate(flops=600 * 10**6, bytes_accessed=4 * 10**6, transcendentals=nodes * hidden_width),
        name="layer",
    )(recv, adj, w_in, bias.reshape(1, hidden_width), cotangent)

    pieces = lax.all_to_all(terms.reshape(feat_size, width, hidden_width), "feat", split_axis=0, concat_axis=0, tiled=True)
    mine = jnp.sum(pieces, axis=0)
    copies = jnp.broadcast_to(mine[None], (row_size, width, hidden_width))
    pieces = lax.all_to_all(copies, "rows", split_axis=0, concat_axis=0, tiled=True)
    return hidden, jnp.sum(pieces, axis=0)


def solution(mesh):
    in_specs = (
        P("feat", None, "rows"),
        P(),
        P(),
        P(("feat", "rows"), None, None, None),
        P(("feat", "rows"), None),
        P(("feat", "rows")),
        P(("feat", "rows"), None),
    )
    out_specs = (P(("feat", "rows"), None), P("feat", None))
    return jax.shard_map(body, mesh=mesh, in_specs=in_specs, out_specs=out_specs, check_vma=False)
```

time: 217 us -> 52.5 us (0.24)
  blocking collectives: 90.9 us -> 20.1 us
  waiting for transfers between devices: 63.2 us -> 10.9 us
  between operations: 14.2 us -> 0.76 us
  matrix products: 11.6 us -> 0 us
  starting transfers between devices: 22 us -> 11.1 us
  local copies, waits for them, and re-layouts: 9.55 us -> 2.94 us
  Pallas kernels: 0 us -> 4.45 us
  other arithmetic: 5.11 us -> 1.94 us
    psum x1 -> x0, blocking collectives: 74.5 us -> none  [body(): weight_grad = lax.psum(grad_slice, 'rows')]
    all_gather x1 -> x0, waiting for transfers between devices: 24 us -> none  [body(): lax.all_gather(pieces, 'feat', axis=0, tiled=True)]
    all_to_all x1, waiting for transfers between devices: 33.8 us -> 10.9 us  [body(): lax.all_to_all(send, ('feat', 'rows'), split_axis=0, concat_axis=0, tiled...]
    dot_general x5 -> x0, matrix products: 11.6 us -> none  [the longest x1 3.08 us: body(): jnp.einsum('bkq,bkij->qbij', onehot, masked, preferred_element_type=jnp.f...]
    ppermute x4 -> x0, starting transfers between devices: 10.8 us -> none  [the longest x2 5.42 us: shifted(): return lax.ppermute(block, axis, route)]
    ppermute x4 -> x0, waiting for transfers between devices: 5.31 us -> none  [the longest x1 2.85 us: padded(): lax.ppermute(tail, axis, [(i, (i + 1) % count) for i in range(count)])]
    pallas_call x0 -> x2, Pallas kernels: none -> 4.45 us  [the longest x1 3.18 us: body(): pl.pallas_call(layer_kernel, out_shape=(jax.ShapeDtypeStruct((nodes, hidd...]
    all_to_all x1 -> x2, blocking collectives: 16.3 us -> 20.1 us  [the longest x1 11.6 us: body(): lax.all_to_all(copies, 'rows', split_axis=0, concat_axis=0, tiled=True)]
  transfers between devices with their start and end apart: 6 -> 1, of which waited for: 5 -> 1; matrix products, arithmetic and copies ran while one was open for 3% -> 0% of each run, Pallas kernels for 0% -> 2%
where the time goes in v1:
time: 52.5 us; the launch traced here: 52.3 us
  blocking collectives  20.1 us (38%)
  starting transfers between devices  11.1 us (21%)
  waiting for transfers between devices  10.9 us (21%)
  Pallas kernels  4.45 us (8%)
  local copies, waits for them, and re-layouts  2.94 us (6%)
  other arithmetic  1.94 us (4%)
  between operations  0.76 us (1%)
    all_to_all x1, blocking collectives, body(): lax.all_to_all(copies, 'rows', split_axis=0, concat_axis=0, tiled=True)  11.6 us
    all_to_all x1, starting transfers between devices, body(): lax.all_to_all(send, ('feat', 'rows'), split_axis=0, concat_axis=0, tiled...  11.1 us
    all_to_all x1, waiting for transfers between devices, body(): lax.all_to_all(send, ('feat', 'rows'), split_axis=0, concat_axis=0, tiled...  10.9 us
    all_to_all x1, blocking collectives, body(): lax.all_to_all(terms.reshape(feat_size, width, hidden_width), 'feat', spl...  8.51 us
    pallas_call x1, Pallas kernels, body(): pl.pallas_call(layer_kernel, out_shape=(jax.ShapeDtypeStruct((nodes, hidd...  3.18 us
    unnamed x13, local copies, waits for them, and re-layouts  2.78 us
    pallas_call x1, Pallas kernels, body(): pl.pallas_call(lambda *refs: adjacency_kernel(*refs, rows_axis='rows', cy...  1.26 us
    concatenate x1, other arithmetic, body(): send = jnp.concatenate([by_owner, beside.reshape(by_owner.shape)], axis=2)  1.08 us
  transfers between devices with their start and end apart: 1, of which 1 were waited for; matrix products, arithmetic and copies ran while one was open for 0% of the time, Pallas kernels for 2%

profile of v1, /device:TPU:0, one launch (start us, length us, event | category | flops | bytes accessed | tf_op | source)
XLA Modules:
  0.0 52.3 jit_solution(15678746416104223786)
XLA Ops:
  0.6 1.3 %copy.11 = bf16[16,128,48]{2,0,1:T(8,128)(2,1)S(1)} copy(bf16[16,128,48]{1,2,0:T(8,128)(2,1)} %param.7) | data formatting | bytes 393216 | tf_op args[0]
  2.0 0.1 fusion.1
  2.1 0.0 copy-start.3
  2.2 0.0 copy-start.5
  2.2 0.2 maximum_select_fusion
  2.4 1.1 %pad_maximum_fusion = bf16[128,16,96]{2,1,0:T(8,128)(2,1)} fusion(bf16[128,16,48]{2,1,0:T(8,128)(2,1)S(1)} %bitcast.14, bf16[128,16,48]{2,1,0:T(8,128)(2,1)S(1)} %bitcast.13), kind=kLoop, calls=%fused_computation.1 | loop fusion | flops 786432 | bytes 786432 | tf_op jit(solution)/shard_map/concatenate | solution.py:95
  3.5 0.0 copy-start.1
  3.5 0.0 copy-start.2
  3.5 11.1 %all-to-all-start = ((bf16[128,16,96]{2,1,0:T(8,128)(2,1)}), bf16[128,16,96]{2,1,0:T(8,128)(2,1)S(1)}, u32[]{:S(2)}, u32[]{:S(2)}) async-start(bf16[128,16,96]{2,1,0:T(8,128)(2,1)} %pad_maximum_fusion), calls=%async_computation | async-start | bytes 1048576 | tf_op jit(solution)/shard_map/all_to_all | solution.py:96
  14.6 0.0 copy-start.4
  14.7 0.0 copy-done.3
  14.7 0.0 copy-done.5
  14.7 0.0 copy-start
  14.7 1.4 %copy-done = bf16[6,8,128,128]{3,2,1,0:T(8,128)(2,1)S(1)} copy-done((bf16[6,8,128,128]{3,2,1,0:T(8,128)(2,1)S(1)}, bf16[6,8,128,128]{3,2,1,0:T(8,128)(2,1)}, u32[]{:S(2)}) %copy-start) | copy-done | bytes 1572888
  16.1 1.3 %adjacency.1.adj_ref = bf16[768,1280]{1,0:T(8,128)(2,1)S(1)} custom-call(s32[6,8]{1,0:T(8,128)S(1)} %copy-done.3, s32[6]{0:T(128)S(1)} %copy-done.5, s32[1]{0:T(128)} %bitcast.5.refs_2_, bf16[6,8,128,128]{3,2,1,0:T(8,128)(2,1)S(1)} %copy-done), custom_call_target="tpu_custom_call" | custom-call | flops 2000000 | bytes 4000000 | tf_op jit(solution)/shard_map/adjacency/pallas_call | solution.py:103
  17.4 10.9 %all-to-all-done = bf16[128,16,96]{2,1,0:T(8,128)(2,1)S(1)} async-done(((bf16[128,16,96]{2,1,0:T(8,128)(2,1)}), bf16[128,16,96]{2,1,0:T(8,128)(2,1)S(1)}, u32[]{:S(2)}, u32[]{:S(2)}) %all-to-all-start) | async-done | bytes 393248 | tf_op jit(solution)/shard_map/all_to_all | solution.py:96
  28.2 0.0 copy-done.1
  28.2 0.0 copy-done.2
  28.3 0.0 copy-done.4
  28.3 3.2 %layer.1 = (bf16[768,256]{1,0:T(8,128)(2,1)}, f32[128,256]{1,0:T(8,128)S(1)}) custom-call(bf16[8,16,16,96]{3,2,1,0:T(8,128)(2,1)S(1)} %bitcast.8, bf16[768,1280]{1,0:T(8,128)(2,1)S(1)} %adjacency.1.adj_ref, bf16[128,256]{1,0:T(8,128)(2,1)S(1)} %copy-done.2, f32[1,256]{1,0:T(1,128)S(1)} %bitcast.10, bf16[768,256]{1,0:T(8,128)(2,1)S(1)} %copy-done.1), custom_call_target="tpu_custom_call" | custom-call | flops 600000000 | bytes 4000000 | tf_op jit(solution)/shard_map/layer/pallas_call | solution.py:112
  31.4 8.5 %all_to_all.15 = f32[8,16,256]{2,1,0:T(8,128)S(1)} all-to-all(f32[8,16,256]{2,1,0:T(8,128)S(1)} %bitcast.9), channel_id=1, replica_groups=mesh['feat'=8,'rows'=16] {'feat'}, dimensions={0} | all-to-all | bytes 262144 | tf_op jit(solution)/shard_map/all_to_all | solution.py:126
  40.0 11.6 %all_to_all.16 = f32[16,16,256]{2,1,0:T(8,128)S(1)} all-to-all(f32[16,16,256]{2,1,0:T(8,128)S(1)} %broadcast_in_dim.2), channel_id=1, replica_groups=mesh['feat'=8,'rows'=16] {'rows'}, dimensions={0} | all-to-all | bytes 524288 | tf_op jit(solution)/shard_map/all_to_all | solution.py:129
  51.6 0.6 %reduce_sum.19 = f32[16,256]{1,0:T(8,128)} reduce(f32[16,16,256]{2,1,0:T(8,128)S(1)} %all_to_all.16, f32[]{:T(128)} %constant.18.clone.1), dimensions={0}, to_apply=%region_1.2 | reduce | flops 61440 | bytes 278532 | tf_op jit(solution)/shard_map/reduce_sum | solution.py:130
  (3 shorter events, 0.0 us)
Async XLA Ops:
  2.1 12.5 %copy-start.3 = (s32[6,8]{1,0:T(8,128)S(1)}, s32[6,8]{1,0:T(8,128)}, u32[]{:S(2)}) copy-start(s32[6,8]{1,0:T(8,128)} %refs_0_.1) | copy-start | bytes 580
  2.2 12.5 %copy-start.5 = (s32[6]{0:T(128)S(1)}, s32[6]{0:T(128)}, u32[]{:S(2)}) copy-start(s32[6]{0:T(128)} %refs_1_.1) | copy-start | bytes 76
  3.5 24.8 %copy-start.1 = (bf16[768,256]{1,0:T(8,128)(2,1)S(1)}, bf16[768,256]{1,0:T(8,128)(2,1)}, u32[]{:S(2)}) copy-start(bf16[768,256]{1,0:T(8,128)(2,1)} %cot_ref.1) | copy-start | bytes 1179652
  3.5 24.8 %copy-start.2 = (bf16[128,256]{1,0:T(8,128)(2,1)S(1)}, bf16[128,256]{1,0:T(8,128)(2,1)}, u32[]{:S(2)}) copy-start(bf16[128,256]{1,0:T(8,128)(2,1)} %w_ref.1) | copy-start | bytes 196612
  3.5 24.8 %all-to-all-start = ((bf16[128,16,96]{2,1,0:T(8,128)(2,1)}), bf16[128,16,96]{2,1,0:T(8,128)(2,1)S(1)}, u32[]{:S(2)}, u32[]{:S(2)}) async-start(bf16[128,16,96]{2,1,0:T(8,128)(2,1)} %pad_maximum_fusion), calls=%async_computation | async-start | bytes 1048576 | tf_op jit(solution)/shard_map/all_to_all | solution.py:96
  14.6 13.6 %copy-start.4 = (f32[256]{0:T(256)S(1)}, f32[256]{0:T(256)}, u32[]{:S(2)}) copy-start(f32[256]{0:T(256)} %param.9) | copy-start | bytes 3076
  14.7 1.4 %copy-start = (bf16[6,8,128,128]{3,2,1,0:T(8,128)(2,1)S(1)}, bf16[6,8,128,128]{3,2,1,0:T(8,128)(2,1)}, u32[]{:S(2)}) copy-start(bf16[6,8,128,128]{3,2,1,0:T(8,128)(2,1)} %refs_3_.1) | copy-start | bytes 4718596

commit v2 on v1

--- a/solution.py
+++ b/solution.py
@@ -6,11 +6,14 @@
 from jax.sharding import PartitionSpec as P
 
 HALO_BLK = 2
+LANES = 128
+CHUNK = 256
+GELU_A, GELU_B = 0.7978845608, 0.044715
 F32 = jnp.float32
 BF16 = jnp.bfloat16
 
 
-def adjacency_kernel(cols_ref, counts_ref, base_ref, tiles_ref, adj_ref, *, rows_axis, cycle):
+def adjacency_kernel(cols_ref, counts_ref, base_ref, tiles_ref, adj_ref, *, cycle):
     nb, slots, side, _ = tiles_ref.shape
     adj_ref[...] = jnp.zeros_like(adj_ref)
     eye = (
@@ -31,6 +34,25 @@
                 adj_ref[at] = adj_ref[at] + tiles_ref[b, k]
 
 
+def send_kernel(step_ref, x_ref, out_ref, rows_ref, *, ring):
+    width, part, owners = x_ref.shape
+    i = lax.broadcasted_iota(jnp.int32, (owners, owners), 0)
+    k = lax.broadcasted_iota(jnp.int32, (owners, owners), 1)
+    beside = (i // ring) * ring + lax.rem(lax.rem(i, ring) + step_ref[0] + ring, ring)
+    pick = jnp.concatenate([jnp.where(k == i, 1.0, 0.0), jnp.where(k == beside, 1.0, 0.0)], axis=1).astype(BF16)
+    none = jnp.zeros((part, owners), BF16)
+    rest = jnp.zeros((LANES - 2 * part, 2 * owners), BF16)
+    for c in range(width):
+        x = x_ref[c]
+        spread = jnp.concatenate(
+            [jnp.concatenate([x, none], axis=1), jnp.concatenate([none, x], axis=1), rest], axis=0
+        )
+        rows_ref[pl.ds(c, owners, stride=width), :] = lax.dot_general(
+            pick, spread, (((1,), (1,)), ((), ())), preferred_element_type=F32
+        )
+    out_ref[...] = rows_ref[...].astype(BF16).reshape(out_ref.shape)
+
+
 def layer_kernel(recv_ref, adj_ref, w_ref, bias_ref, cot_ref, hidden_ref, grad_ref, x_ref):
     groups, senders, width, lanes = recv_ref.shape
     features = groups * width
@@ -40,8 +62,7 @@
     part = nodes // senders
     x_ref[:, features:] = jnp.ones((ext, features), BF16)
     for r in range(senders):
-        piece = recv_ref[:, r].reshape(features, lanes)
-        piece = jnp.concatenate([piece, jnp.zeros((features, 128 - lanes), BF16)], axis=1).T
+        piece = recv_ref[:, r].reshape(features, lanes).T
         x_ref[halo + r * part : halo + (r + 1) * part, :features] = piece[:part]
         first, last = r * part, (r + 1) * part
         if first < halo:
@@ -54,11 +75,10 @@
     w = w_ref[...]
     ww = jnp.concatenate([w, w], axis=0)
     bias = bias_ref[...]
-    side = 128
     hidden_width = w.shape[1]
     total = jnp.zeros((2 * features, hidden_width), F32)
-    for b in range(nodes // side):
-        rows = pl.ds(b * side, side)
+    for b in range(nodes // CHUNK):
+        rows = pl.ds(b * CHUNK, CHUNK)
         both = jnp.dot(adj_ref[rows, :], x_ref[...], preferred_element_type=F32)
         y = both[:, :features]
         inv = 1.0 / both[:, features:]
@@ -68,11 +88,12 @@
         yy = jnp.concatenate([y_hi, y_lo], axis=1)
         v = jnp.dot(yy, ww, preferred_element_type=F32) * inv + bias
         v2 = v * v
-        t = jnp.tanh(0.7978845608 * (v + 0.044715 * v2 * v))
-        half = 0.5 * (1.0 + t)
-        hidden_ref[rows, :] = (v * half).astype(BF16)
-        slope = half + 0.5 * v * (1.0 - t * t) * 0.7978845608 * (1.0 + 3.0 * 0.044715 * v2)
-        scaled = (cot_ref[rows, :].astype(F32) * slope * inv).astype(BF16)
+        t = jnp.tanh(v * (GELU_A + (GELU_A * GELU_B) * v2))
+        half = 0.5 + 0.5 * t
+        h = v * half
+        hidden_ref[rows, :] = h.astype(BF16)
+        slope = half + h * (1.0 - t) * (GELU_A + (3.0 * GELU_A * GELU_B) * v2)
+        scaled = (cot_ref[rows, :].astype(F32) * inv * slope).astype(BF16)
         total += lax.dot_general(yy, scaled, (((0,), (0,)), ((), ())), preferred_element_type=F32)
     grad_ref[...] = total[:features] + total[features:]
 
@@ -89,19 +110,25 @@
     row_id = lax.axis_index("rows")
     cycle = block_rows * row_size
 
-    by_owner = features.transpose(1, 0, 2)
-    ring = by_owner.reshape(feat_size, row_size, width, part)
-    beside = jnp.where(row_id * 2 < row_size, jnp.roll(ring, -1, axis=1), jnp.roll(ring, 1, axis=1))
-    send = jnp.concatenate([by_owner, beside.reshape(by_owner.shape)], axis=2)
+    vmem = pl.BlockSpec(memory_space=pltpu.VMEM)
+    smem = pl.BlockSpec(memory_space=pltpu.SMEM)
+    step = jnp.where(row_id * 2 < row_size, 1, -1).reshape(1).astype(jnp.int32)
+    send = pl.pallas_call(
+        lambda *refs: send_kernel(*refs, ring=row_size),
+        out_shape=jax.ShapeDtypeStruct((owners, width, LANES), BF16),
+        in_specs=[smem, vmem],
+        out_specs=vmem,
+        scratch_shapes=[pltpu.VMEM((owners * width, LANES), F32)],
+        compiler_params=pltpu.CompilerParams(vmem_limit_bytes=8 * 2**20),
+        name="pieces",
+    )(step, features.transpose(0, 2, 1))
     recv = lax.all_to_all(send, ("feat", "rows"), split_axis=0, concat_axis=0, tiled=True)
-    recv = recv.reshape(feat_size, row_size, width, 2 * part)
+    recv = recv.reshape(feat_size, row_size, width, LANES)
 
     base = (feat_id * cycle + row_id * block_rows).reshape(1).astype(jnp.int32)
     ext = nodes + 2 * halo
-    vmem = pl.BlockSpec(memory_space=pltpu.VMEM)
-    smem = pl.BlockSpec(memory_space=pltpu.SMEM)
     adj = pl.pallas_call(
-        lambda *refs: adjacency_kernel(*refs, rows_axis="rows", cycle=cycle),
+        lambda *refs: adjacency_kernel(*refs, cycle=cycle),
         out_shape=jax.ShapeDtypeStruct((nodes, ext), BF16),
         in_specs=[smem, smem, smem, vmem],
         out_specs=vmem,

time: 52.5 us -> 51.3 us (0.977)
  waiting for transfers between devices: 10.9 us -> 9.55 us
  other arithmetic: 1.94 us -> 0.64 us
  local copies, waits for them, and re-layouts: 2.94 us -> 3.7 us
  Pallas kernels: 4.45 us -> 5.14 us
    pallas_call x1 -> x2, Pallas kernels: 1.26 us -> 2.68 us  [the longest x1 1.4 us: body(): pl.pallas_call(lambda *refs: send_kernel(*refs, ring=row_size), out_shape...]
    all_to_all x1, waiting for transfers between devices: 10.9 us -> 9.55 us  [body(): lax.all_to_all(send, ('feat', 'rows'), split_axis=0, concat_axis=0, tiled...]
    concatenate x1 -> x0, other arithmetic: 1.08 us -> none  [body(): send = jnp.concatenate([by_owner, beside.reshape(by_owner.shape)], axis=2)]
    unnamed x13 -> x14, local copies, waits for them, and re-layouts: 2.78 us -> 3.68 us
    pallas_call x1, Pallas kernels: 3.18 us -> 2.46 us  [body(): pl.pallas_call(layer_kernel, out_shape=(jax.ShapeDtypeStruct((nodes, hidd...]
  transfers between devices with their start and end apart: 1 -> 1, of which waited for: 1 -> 1; matrix products, arithmetic and copies ran while one was open for 0% -> 0% of each run, Pallas kernels for 2% -> 3%
where the time goes in v2:
time: 51.3 us; the launch traced here: 51 us
  blocking collectives  20.1 us (39%)
  starting transfers between devices  11.1 us (22%)
  waiting for transfers between devices  9.55 us (19%)
  Pallas kernels  5.14 us (10%)
  local copies, waits for them, and re-layouts  3.7 us (7%)
  between operations  0.7 us (1%)
  other arithmetic  0.64 us (1%)
    all_to_all x1, blocking collectives, body(): lax.all_to_all(copies, 'rows', split_axis=0, concat_axis=0, tiled=True)  11.6 us
    all_to_all x1, starting transfers between devices, body(): lax.all_to_all(send, ('feat', 'rows'), split_axis=0, concat_axis=0, tiled...  11.1 us
    all_to_all x1, waiting for transfers between devices, body(): lax.all_to_all(send, ('feat', 'rows'), split_axis=0, concat_axis=0, tiled...  9.55 us
    all_to_all x1, blocking collectives, body(): lax.all_to_all(terms.reshape(feat_size, width, hidden_width), 'feat', spl...  8.51 us
    unnamed x14, local copies, waits for them, and re-layouts  3.68 us
    pallas_call x1, Pallas kernels, body(): pl.pallas_call(layer_kernel, out_shape=(jax.ShapeDtypeStruct((nodes, hidd...  2.46 us
    pallas_call x1, Pallas kernels, body(): pl.pallas_call(lambda *refs: send_kernel(*refs, ring=row_size), out_shape...  1.4 us
    pallas_call x1, Pallas kernels, body(): pl.pallas_call(lambda *refs: adjacency_kernel(*refs, cycle=cycle), out_sh...  1.28 us
  transfers between devices with their start and end apart: 1, of which 1 were waited for; matrix products, arithmetic and copies ran while one was open for 0% of the time, Pallas kernels for 3%

profile of v2, /device:TPU:0, one launch (start us, length us, event | category | flops | bytes accessed | tf_op | source)
XLA Modules:
  0.0 51.0 jit_solution(18146681998151368981)
XLA Ops:
  0.6 0.0 copy-start.2
  0.6 0.9 %copy-done.2 = bf16[16,128,48]{1,2,0:T(8,128)(2,1)S(1)} copy-done((bf16[16,128,48]{1,2,0:T(8,128)(2,1)S(1)}, bf16[16,128,48]{1,2,0:T(8,128)(2,1)}, u32[]{:S(2)}) %copy-start.2) | copy-done | bytes 196632
  1.6 1.4 %pieces.1 = bf16[128,16,128]{2,1,0:T(8,128)(2,1)} custom-call(s32[1]{0:T(128)} %bitcast.refs_0_, bf16[16,48,128]{2,1,0:T(8,128)(2,1)S(1)} %bitcast.7), custom_call_target="tpu_custom_call" | custom-call | tf_op jit(solution)/shard_map/pieces/pallas_call | solution.py:116
  3.0 0.0 copy-start.1
  3.0 0.0 copy-start.3
  3.0 11.1 %all-to-all-start = ((bf16[128,16,128]{2,1,0:T(8,128)(2,1)}), bf16[128,16,128]{2,1,0:T(8,128)(2,1)S(1)}, u32[]{:S(2)}, u32[]{:S(2)}) async-start(bf16[128,16,128]{2,1,0:T(8,128)(2,1)} %pieces.1), calls=%async_computation | async-start | bytes 1048576 | tf_op jit(solution)/shard_map/all_to_all | solution.py:125
  14.1 0.0 copy-start.5
  14.1 0.0 copy-start
  14.1 1.4 %copy-done = bf16[6,8,128,128]{3,2,1,0:T(8,128)(2,1)S(1)} copy-done((bf16[6,8,128,128]{3,2,1,0:T(8,128)(2,1)S(1)}, bf16[6,8,128,128]{3,2,1,0:T(8,128)(2,1)}, u32[]{:S(2)}) %copy-start) | copy-done | bytes 1572888
  15.5 0.0 copy-start.4
  15.6 0.7 %copy-done.4 = s32[6,8]{1,0:T(8,128)S(1)} copy-done((s32[6,8]{1,0:T(8,128)S(1)}, s32[6,8]{1,0:T(8,128)}, u32[]{:S(2)}) %copy-start.4) | copy-done | bytes 216
  16.2 0.0 copy-start.6
  16.2 0.7 %copy-done.6 = s32[6]{0:T(128)S(1)} copy-done((s32[6]{0:T(128)S(1)}, s32[6]{0:T(128)}, u32[]{:S(2)}) %copy-start.6) | copy-done | bytes 48
  16.9 1.3 %adjacency.1.adj_ref = bf16[768,1280]{1,0:T(8,128)(2,1)S(1)} custom-call(s32[6,8]{1,0:T(8,128)S(1)} %copy-done.4, s32[6]{0:T(128)S(1)} %copy-done.6, s32[1]{0:T(128)} %bitcast.3.refs_2_, bf16[6,8,128,128]{3,2,1,0:T(8,128)(2,1)S(1)} %copy-done), custom_call_target="tpu_custom_call" | custom-call | flops 2000000 | bytes 4000000 | tf_op jit(solution)/shard_map/adjacency/pallas_call | solution.py:130
  18.2 9.5 %all-to-all-done = bf16[128,16,128]{2,1,0:T(8,128)(2,1)S(1)} async-done(((bf16[128,16,128]{2,1,0:T(8,128)(2,1)}), bf16[128,16,128]{2,1,0:T(8,128)(2,1)S(1)}, u32[]{:S(2)}, u32[]{:S(2)}) %all-to-all-start) | async-done | bytes 524320 | tf_op jit(solution)/shard_map/all_to_all | solution.py:125
  27.7 0.0 copy-done.1
  27.7 0.0 copy-done.3
  27.7 0.0 copy-done.5
  27.7 2.5 %layer.1 = (bf16[768,256]{1,0:T(8,128)(2,1)}, f32[128,256]{1,0:T(8,128)S(1)}) custom-call(bf16[8,16,16,128]{3,2,1,0:T(8,128)(2,1)S(1)} %bitcast.6, bf16[768,1280]{1,0:T(8,128)(2,1)S(1)} %adjacency.1.adj_ref, bf16[128,256]{1,0:T(8,128)(2,1)S(1)} %copy-done.3, f32[1,256]{1,0:T(1,128)S(1)} %bitcast.9, bf16[768,256]{1,0:T(8,128)(2,1)S(1)} %copy-done.1), custom_call_target="tpu_custom_call" | custom-call | flops 600000000 | bytes 4000000 | tf_op jit(solution)/shard_map/layer/pallas_call | solution.py:139
  30.2 8.5 %all_to_all.15 = f32[8,16,256]{2,1,0:T(8,128)S(1)} all-to-all(f32[8,16,256]{2,1,0:T(8,128)S(1)} %bitcast.8), channel_id=1, replica_groups=mesh['feat'=8,'rows'=16] {'feat'}, dimensions={0} | all-to-all | bytes 262144 | tf_op jit(solution)/shard_map/all_to_all | solution.py:153
  38.7 11.6 %all_to_all.16 = f32[16,16,256]{2,1,0:T(8,128)S(1)} all-to-all(f32[16,16,256]{2,1,0:T(8,128)S(1)} %broadcast_in_dim.2), channel_id=1, replica_groups=mesh['feat'=8,'rows'=16] {'rows'}, dimensions={0} | all-to-all | bytes 524288 | tf_op jit(solution)/shard_map/all_to_all | solution.py:156
  50.4 0.6 %reduce_sum.19 = f32[16,256]{1,0:T(8,128)} reduce(f32[16,16,256]{2,1,0:T(8,128)S(1)} %all_to_all.16, f32[]{:T(128)} %constant.22.clone.1), dimensions={0}, to_apply=%region_1.2 | reduce | flops 61440 | bytes 278532 | tf_op jit(solution)/shard_map/reduce_sum | solution.py:157
  (2 shorter events, 0.0 us)
Async XLA Ops:
  0.6 0.9 %copy-start.2 = (bf16[16,128,48]{1,2,0:T(8,128)(2,1)S(1)}, bf16[16,128,48]{1,2,0:T(8,128)(2,1)}, u32[]{:S(2)}) copy-start(bf16[16,128,48]{1,2,0:T(8,128)(2,1)} %param.7) | copy-start | bytes 589828
  3.0 24.8 %copy-start.1 = (bf16[768,256]{1,0:T(8,128)(2,1)S(1)}, bf16[768,256]{1,0:T(8,128)(2,1)}, u32[]{:S(2)}) copy-start(bf16[768,256]{1,0:T(8,128)(2,1)} %cot_ref.1) | copy-start | bytes 1179652
  3.0 24.8 %copy-start.3 = (bf16[128,256]{1,0:T(8,128)(2,1)S(1)}, bf16[128,256]{1,0:T(8,128)(2,1)}, u32[]{:S(2)}) copy-start(bf16[128,256]{1,0:T(8,128)(2,1)} %w_ref.1) | copy-start | bytes 196612
  3.0 24.8 %all-to-all-start = ((bf16[128,16,128]{2,1,0:T(8,128)(2,1)}), bf16[128,16,128]{2,1,0:T(8,128)(2,1)S(1)}, u32[]{:S(2)}, u32[]{:S(2)}) async-start(bf16[128,16,128]{2,1,0:T(8,128)(2,1)} %pieces.1), calls=%async_computation | async-start | bytes 1048576 | tf_op jit(solution)/shard_map/all_to_all | solution.py:125
  14.1 13.6 %copy-start.5 = (f32[256]{0:T(256)S(1)}, f32[256]{0:T(256)}, u32[]{:S(2)}) copy-start(f32[256]{0:T(256)} %param.9) | copy-start | bytes 3076
  14.1 1.4 %copy-start = (bf16[6,8,128,128]{3,2,1,0:T(8,128)(2,1)S(1)}, bf16[6,8,128,128]{3,2,1,0:T(8,128)(2,1)}, u32[]{:S(2)}) copy-start(bf16[6,8,128,128]{3,2,1,0:T(8,128)(2,1)} %refs_3_.1) | copy-start | bytes 4718596
  15.5 0.7 %copy-start.4 = (s32[6,8]{1,0:T(8,128)S(1)}, s32[6,8]{1,0:T(8,128)}, u32[]{:S(2)}) copy-start(s32[6,8]{1,0:T(8,128)} %refs_0_.1) | copy-start | bytes 580
  16.2 0.7 %copy-start.6 = (s32[6]{0:T(128)S(1)}, s32[6]{0:T(128)}, u32[]{:S(2)}) copy-start(s32[6]{0:T(128)} %refs_1_.1) | copy-start | bytes 76

commit v3 on v2

--- a/solution.py
+++ b/solution.py
@@ -7,6 +7,9 @@
 
 HALO_BLK = 2
 LANES = 128
+CORES = 2
+FEAT = ("x", "core")
+ALL = ("x", "core", "rows")
 CHUNK = 256
 GELU_A, GELU_B = 0.7978845608, 0.044715
 F32 = jnp.float32
@@ -53,7 +56,7 @@
     out_ref[...] = rows_ref[...].astype(BF16).reshape(out_ref.shape)
 
 
-def layer_kernel(recv_ref, adj_ref, w_ref, bias_ref, cot_ref, hidden_ref, grad_ref, x_ref):
+def layer_kernel(recv_ref, adj_ref, w_ref, bias_ref, cot_ref, core_ref, hidden_ref, mine_ref, other_ref, x_ref):
     groups, senders, width, lanes = recv_ref.shape
     features = groups * width
     nodes = hidden_ref.shape[0]
@@ -95,18 +98,22 @@
         slope = half + h * (1.0 - t) * (GELU_A + (3.0 * GELU_A * GELU_B) * v2)
         scaled = (cot_ref[rows, :].astype(F32) * inv * slope).astype(BF16)
         total += lax.dot_general(yy, scaled, (((0,), (0,)), ((), ())), preferred_element_type=F32)
-    grad_ref[...] = total[:features] + total[features:]
+    total = total[:features] + total[features:]
+    total = total.reshape(mine_ref.shape[0], CORES, width, hidden_width)
+    first = core_ref[0] == 0
+    mine_ref[...] = jnp.where(first, total[:, 0], total[:, 1])
+    other_ref[...] = jnp.where(first, total[:, 1], total[:, 0])
 
 
 def body(features, w_in, bias, tiles, tile_cols, tile_counts, cotangent):
     block_rows, slots, side, _ = tiles.shape
     n_features, hidden_width = w_in.shape
-    feat_size = lax.axis_size("feat")
+    feat_size = lax.axis_size(FEAT)
     row_size = lax.axis_size("rows")
     nodes = block_rows * side
     halo = HALO_BLK * side
     width, owners, part = features.shape
-    feat_id = lax.axis_index("feat")
+    feat_id = lax.axis_index(FEAT)
     row_id = lax.axis_index("rows")
     cycle = block_rows * row_size
 
@@ -122,7 +129,7 @@
         compiler_params=pltpu.CompilerParams(vmem_limit_bytes=8 * 2**20),
         name="pieces",
     )(step, features.transpose(0, 2, 1))
-    recv = lax.all_to_all(send, ("feat", "rows"), split_axis=0, concat_axis=0, tiled=True)
+    recv = lax.all_to_all(send, ALL, split_axis=0, concat_axis=0, tiled=True)
     recv = recv.reshape(feat_size, row_size, width, LANES)
 
     base = (feat_id * cycle + row_id * block_rows).reshape(1).astype(jnp.int32)
@@ -136,36 +143,37 @@
         cost_estimate=pl.CostEstimate(flops=2 * 10**6, bytes_accessed=4 * 10**6, transcendentals=0),
         name="adjacency",
     )(tile_cols, tile_counts, base, tiles)
-    hidden, terms = pl.pallas_call(
+    chips = feat_size // CORES
+    half = jax.ShapeDtypeStruct((chips, width, hidden_width), F32)
+    hidden, mine, other = pl.pallas_call(
         layer_kernel,
-        out_shape=(
-            jax.ShapeDtypeStruct((nodes, hidden_width), BF16),
-            jax.ShapeDtypeStruct((n_features, hidden_width), F32),
-        ),
-        in_specs=[vmem] * 5,
-        out_specs=(vmem, vmem),
+        out_shape=(jax.ShapeDtypeStruct((nodes, hidden_width), BF16), half, half),
+        in_specs=[vmem] * 5 + [smem],
+        out_specs=(vmem, vmem, vmem),
         scratch_shapes=[pltpu.VMEM((ext, 2 * n_features), BF16)],
         compiler_params=pltpu.CompilerParams(vmem_limit_bytes=24 * 2**20),
         cost_estimate=pl.CostEstimate(flops=600 * 10**6, bytes_accessed=4 * 10**6, transcendentals=nodes * hidden_width),
         name="layer",
-    )(recv, adj, w_in, bias.reshape(1, hidden_width), cotangent)
+    )(recv, adj, w_in, bias.reshape(1, hidden_width), cotangent, lax.axis_index("core").reshape(1))
 
-    pieces = lax.all_to_all(terms.reshape(feat_size, width, hidden_width), "feat", split_axis=0, concat_axis=0, tiled=True)
-    mine = jnp.sum(pieces, axis=0)
-    copies = jnp.broadcast_to(mine[None], (row_size, width, hidden_width))
-    pieces = lax.all_to_all(copies, "rows", split_axis=0, concat_axis=0, tiled=True)
-    return hidden, jnp.sum(pieces, axis=0)
+    pair = (mine + lax.ppermute(other, "core", [(0, 1), (1, 0)])).astype(BF16)
+    copies = jnp.broadcast_to(pair[:, None], (chips, row_size, width, hidden_width))
+    copies = copies.reshape(chips * row_size, width, hidden_width)
+    pieces = lax.all_to_all(copies, ("x", "rows"), split_axis=0, concat_axis=0, tiled=True)
+    return hidden, jnp.sum(pieces.astype(F32), axis=0)
 
 
 def solution(mesh):
+    devices = mesh.devices
+    mesh = jax.sharding.Mesh(devices.reshape(devices.shape[0] // CORES, CORES, devices.shape[1]), ALL)
     in_specs = (
-        P("feat", None, "rows"),
+        P(FEAT, None, "rows"),
         P(),
         P(),
-        P(("feat", "rows"), None, None, None),
-        P(("feat", "rows"), None),
-        P(("feat", "rows")),
-        P(("feat", "rows"), None),
+        P(ALL, None, None, None),
+        P(ALL, None),
+        P(ALL),
+        P(ALL, None),
     )
-    out_specs = (P(("feat", "rows"), None), P("feat", None))
+    out_specs = (P(ALL, None), P(FEAT, None))
     return jax.shard_map(body, mesh=mesh, in_specs=in_specs, out_specs=out_specs, check_vma=False)

time: 51.3 us -> 50.5 us (0.984)
  blocking collectives: 20.1 us -> 18 us
  waiting for transfers between devices: 9.55 us -> 10.5 us
    all_to_all x2 -> x1, blocking collectives: 20.1 us -> 18 us  [body(): lax.all_to_all(copies, ('x', 'rows'), split_axis=0, concat_axis=0, tiled=...]
    ppermute x0 -> x1, waiting for transfers between devices: none -> 1.25 us  [body(): pair = (mine + lax.ppermute(other, 'core', [(0, 1), (1, 0)])).astype(BF16)]
  transfers between devices with their start and end apart: 1 -> 2, of which waited for: 1 -> 2; matrix products, arithmetic and copies ran while one was open for 0% -> 0% of each run, Pallas kernels for 3% -> 3%
where the time goes in v3:
time: 50.5 us; the launch traced here: 50.2 us
  blocking collectives  18 us (36%)
  starting transfers between devices  11.1 us (22%)
  waiting for transfers between devices  10.5 us (21%)
  Pallas kernels  5.43 us (11%)
  local copies, waits for them, and re-layouts  3.71 us (7%)
  other arithmetic  0.71 us (1%)
  between operations  0.71 us (1%)
    all_to_all x1, blocking collectives, body(): lax.all_to_all(copies, ('x', 'rows'), split_axis=0, concat_axis=0, tiled=...  18 us
    all_to_all x1, starting transfers between devices, body(): recv = lax.all_to_all(send, ALL, split_axis=0, concat_axis=0, tiled=True)  11.1 us
    all_to_all x1, waiting for transfers between devices, body(): recv = lax.all_to_all(send, ALL, split_axis=0, concat_axis=0, tiled=True)  9.26 us
    unnamed x14, local copies, waits for them, and re-layouts  3.68 us
    pallas_call x1, Pallas kernels, body(): pl.pallas_call(layer_kernel, out_shape=(jax.ShapeDtypeStruct((nodes, hidd...  2.46 us
    pallas_call x1, Pallas kernels, body(): pl.pallas_call(lambda *refs: adjacency_kernel(*refs, cycle=cycle), out_sh...  1.56 us
    pallas_call x1, Pallas kernels, body(): pl.pallas_call(lambda *refs: send_kernel(*refs, ring=row_size), out_shape...  1.41 us
    ppermute x1, waiting for transfers between devices, body(): pair = (mine + lax.ppermute(other, 'core', [(0, 1), (1, 0)])).astype(BF16)  1.25 us
  transfers between devices with their start and end apart: 2, of which 2 were waited for; matrix products, arithmetic and copies ran while one was open for 0% of the time, Pallas kernels for 3%

profile of v3, /device:TPU:0, one launch (start us, length us, event | category | flops | bytes accessed | tf_op | source)
XLA Modules:
  0.0 50.2 jit_solution(190830995202801505)
XLA Ops:
  0.6 0.0 copy-start.2
  0.6 0.9 %copy-done.2 = bf16[16,128,48]{1,2,0:T(8,128)(2,1)S(1)} copy-done((bf16[16,128,48]{1,2,0:T(8,128)(2,1)S(1)}, bf16[16,128,48]{1,2,0:T(8,128)(2,1)}, u32[]{:S(2)}) %copy-start.2) | copy-done | bytes 196632
  1.6 1.4 %pieces.1 = bf16[128,16,128]{2,1,0:T(8,128)(2,1)} custom-call(s32[1]{0:T(128)} %bitcast.refs_0_, bf16[16,48,128]{2,1,0:T(8,128)(2,1)S(1)} %bitcast.8), custom_call_target="tpu_custom_call" | custom-call | tf_op jit(solution)/shard_map/pieces/pallas_call | solution.py:123
  3.0 0.0 copy-start.1
  3.0 0.0 copy-start.3
  3.0 11.1 %all-to-all-start = ((bf16[128,16,128]{2,1,0:T(8,128)(2,1)}), bf16[128,16,128]{2,1,0:T(8,128)(2,1)S(1)}, u32[]{:S(2)}, u32[]{:S(2)}) async-start(bf16[128,16,128]{2,1,0:T(8,128)(2,1)} %pieces.1), calls=%async_computation | async-start | bytes 1048576 | tf_op jit(solution)/shard_map/all_to_all | solution.py:132
  14.1 0.0 copy-start.5
  14.1 0.0 copy-start
  14.2 1.4 %copy-done = bf16[6,8,128,128]{3,2,1,0:T(8,128)(2,1)S(1)} copy-done((bf16[6,8,128,128]{3,2,1,0:T(8,128)(2,1)S(1)}, bf16[6,8,128,128]{3,2,1,0:T(8,128)(2,1)}, u32[]{:S(2)}) %copy-start) | copy-done | bytes 1572888
  15.6 0.0 copy-start.4
  15.6 0.7 %copy-done.4 = s32[6,8]{1,0:T(8,128)S(1)} copy-done((s32[6,8]{1,0:T(8,128)S(1)}, s32[6,8]{1,0:T(8,128)}, u32[]{:S(2)}) %copy-start.4) | copy-done | bytes 216
  16.2 0.0 copy-start.6
  16.2 0.7 %copy-done.6 = s32[6]{0:T(128)S(1)} copy-done((s32[6]{0:T(128)S(1)}, s32[6]{0:T(128)}, u32[]{:S(2)}) %copy-start.6) | copy-done | bytes 48
  16.9 1.6 %adjacency.1.adj_ref = bf16[768,1280]{1,0:T(8,128)(2,1)S(1)} custom-call(s32[6,8]{1,0:T(8,128)S(1)} %copy-done.4, s32[6]{0:T(128)S(1)} %copy-done.6, s32[1]{0:T(128)} %bitcast.3.refs_2_, bf16[6,8,128,128]{3,2,1,0:T(8,128)(2,1)S(1)} %copy-done), custom_call_target="tpu_custom_call" | custom-call | flops 2000000 | bytes 4000000 | tf_op jit(solution)/shard_map/adjacency/pallas_call | solution.py:137
  18.5 9.3 %all-to-all-done = bf16[128,16,128]{2,1,0:T(8,128)(2,1)S(1)} async-done(((bf16[128,16,128]{2,1,0:T(8,128)(2,1)}), bf16[128,16,128]{2,1,0:T(8,128)(2,1)S(1)}, u32[]{:S(2)}, u32[]{:S(2)}) %all-to-all-start) | async-done | bytes 524320 | tf_op jit(solution)/shard_map/all_to_all | solution.py:132
  27.7 0.0 copy-done.1
  27.7 0.0 copy-done.3
  27.7 0.0 copy-done.5
  27.7 2.5 %layer.1 = (bf16[768,256]{1,0:T(8,128)(2,1)}, f32[4,16,256]{2,1,0:T(8,128)S(1)}, f32[4,16,256]{2,1,0:T(8,128)S(1)}) custom-call(bf16[8,16,16,128]{3,2,1,0:T(8,128)(2,1)S(1)} %bitcast.7, bf16[768,1280]{1,0:T(8,128)(2,1)S(1)} %adjacency.1.adj_ref, bf16[128,256]{1,0:T(8,128)(2,1)S(1)} %copy-done.3, f32[1,256]{1,0:T(1,128)S(1)} %bitcast.9, ...), custom_call_target="tpu_custom_call" | custom-call | flops 600000000 | bytes 4000000 | tf_op jit(solution)/shard_map/layer/pallas_call | solution.py:148
  30.2 0.0 collective-permute-start
  30.2 1.3 %collective-permute-done = f32[4,16,256]{2,1,0:T(8,128)S(1)} collective-permute-done((f32[4,16,256]{2,1,0:T(8,128)S(1)}, f32[4,16,256]{2,1,0:T(8,128)S(1)}, u32[]{:S(2)}, u32[]{:S(2)}) %collective-permute-start) | collective-permute-done | bytes 65568 | tf_op jit(solution)/shard_map/ppermute | solution.py:159
  31.5 18.0 %all_to_all.10 = bf16[64,16,256]{2,1,0:T(8,128)(2,1)S(1)} all-to-all(bf16[64,16,256]{2,1,0:T(8,128)(2,1)S(1)} %bitcast.10), channel_id=1, replica_groups=mesh['x'=4,'core'=2,'rows'=16] {'x','rows'}, dimensions={0} | all-to-all | bytes 1048576 | tf_op jit(solution)/shard_map/all_to_all | solution.py:162
  49.5 0.7 %convert_reduce_fusion = f32[16,256]{1,0:T(8,128)} fusion(bf16[64,16,256]{2,1,0:T(8,128)(2,1)S(1)} %all_to_all.10), kind=kLoop, calls=%fused_computation | loop fusion | flops 520192 | bytes 540672 | tf_op jit(solution)/shard_map/reduce_sum | solution.py:163
  (2 shorter events, 0.0 us)
Async XLA Ops:
  0.6 0.9 %copy-start.2 = (bf16[16,128,48]{1,2,0:T(8,128)(2,1)S(1)}, bf16[16,128,48]{1,2,0:T(8,128)(2,1)}, u32[]{:S(2)}) copy-start(bf16[16,128,48]{1,2,0:T(8,128)(2,1)} %param.7) | copy-start | bytes 589828
  3.0 24.8 %copy-start.1 = (bf16[768,256]{1,0:T(8,128)(2,1)S(1)}, bf16[768,256]{1,0:T(8,128)(2,1)}, u32[]{:S(2)}) copy-start(bf16[768,256]{1,0:T(8,128)(2,1)} %cot_ref.1) | copy-start | bytes 1179652
  3.0 24.8 %copy-start.3 = (bf16[128,256]{1,0:T(8,128)(2,1)S(1)}, bf16[128,256]{1,0:T(8,128)(2,1)}, u32[]{:S(2)}) copy-start(bf16[128,256]{1,0:T(8,128)(2,1)} %w_ref.1) | copy-start | bytes 196612
  3.0 24.8 %all-to-all-start = ((bf16[128,16,128]{2,1,0:T(8,128)(2,1)}), bf16[128,16,128]{2,1,0:T(8,128)(2,1)S(1)}, u32[]{:S(2)}, u32[]{:S(2)}) async-start(bf16[128,16,128]{2,1,0:T(8,128)(2,1)} %pieces.1), calls=%async_computation | async-start | bytes 1048576 | tf_op jit(solution)/shard_map/all_to_all | solution.py:132
  14.1 13.6 %copy-start.5 = (f32[256]{0:T(256)S(1)}, f32[256]{0:T(256)}, u32[]{:S(2)}) copy-start(f32[256]{0:T(256)} %param.9) | copy-start | bytes 3076
  14.1 1.4 %copy-start = (bf16[6,8,128,128]{3,2,1,0:T(8,128)(2,1)S(1)}, bf16[6,8,128,128]{3,2,1,0:T(8,128)(2,1)}, u32[]{:S(2)}) copy-start(bf16[6,8,128,128]{3,2,1,0:T(8,128)(2,1)} %refs_3_.1) | copy-start | bytes 4718596
  15.6 0.7 %copy-start.4 = (s32[6,8]{1,0:T(8,128)S(1)}, s32[6,8]{1,0:T(8,128)}, u32[]{:S(2)}) copy-start(s32[6,8]{1,0:T(8,128)} %refs_0_.1) | copy-start | bytes 580
  16.2 0.7 %copy-start.6 = (s32[6]{0:T(128)S(1)}, s32[6]{0:T(128)}, u32[]{:S(2)}) copy-start(s32[6]{0:T(128)} %refs_1_.1) | copy-start | bytes 76
  30.2 1.3 %collective-permute-start = (f32[4,16,256]{2,1,0:T(8,128)S(1)}, f32[4,16,256]{2,1,0:T(8,128)S(1)}, u32[]{:S(2)}, u32[]{:S(2)}) collective-permute-start(f32[4,16,256]{2,1,0:T(8,128)S(1)} %get-tuple-element.7), channel_id=1, source_target_pairs={{0,16},{16,0},{1,17},{17,1},{2,18},{18,2},{3,19},{19,3},{4,20},{20... | collective-permute-start | bytes 196616 | tf_op jit(solution)/shard_map/ppermute | solution.py:159

commit v4 on v3

--- a/solution.py
+++ b/solution.py
@@ -10,7 +10,7 @@
 CORES = 2
 FEAT = ("x", "core")
 ALL = ("x", "core", "rows")
-CHUNK = 256
+CHUNK = 768
 GELU_A, GELU_B = 0.7978845608, 0.044715
 F32 = jnp.float32
 BF16 = jnp.bfloat16
@@ -94,7 +94,7 @@
         t = jnp.tanh(v * (GELU_A + (GELU_A * GELU_B) * v2))
         half = 0.5 + 0.5 * t
         h = v * half
-        hidden_ref[rows, :] = h.astype(BF16)
+        hidden_ref[rows, :] = h
         slope = half + h * (1.0 - t) * (GELU_A + (3.0 * GELU_A * GELU_B) * v2)
         scaled = (cot_ref[rows, :].astype(F32) * inv * slope).astype(BF16)
         total += lax.dot_general(yy, scaled, (((0,), (0,)), ((), ())), preferred_element_type=F32)
@@ -126,7 +126,7 @@
         in_specs=[smem, vmem],
         out_specs=vmem,
         scratch_shapes=[pltpu.VMEM((owners * width, LANES), F32)],
-        compiler_params=pltpu.CompilerParams(vmem_limit_bytes=8 * 2**20),
+        compiler_params=pltpu.CompilerParams(vmem_limit_bytes=4 * 2**20),
         name="pieces",
     )(step, features.transpose(0, 2, 1))
     recv = lax.all_to_all(send, ALL, split_axis=0, concat_axis=0, tiled=True)
@@ -139,7 +139,7 @@
         out_shape=jax.ShapeDtypeStruct((nodes, ext), BF16),
         in_specs=[smem, smem, smem, vmem],
         out_specs=vmem,
-        compiler_params=pltpu.CompilerParams(vmem_limit_bytes=16 * 2**20),
+        compiler_params=pltpu.CompilerParams(vmem_limit_bytes=2 * 2**20),
         cost_estimate=pl.CostEstimate(flops=2 * 10**6, bytes_accessed=4 * 10**6, transcendentals=0),
         name="adjacency",
     )(tile_cols, tile_counts, base, tiles)
@@ -147,16 +147,18 @@
     half = jax.ShapeDtypeStruct((chips, width, hidden_width), F32)
     hidden, mine, other = pl.pallas_call(
         layer_kernel,
-        out_shape=(jax.ShapeDtypeStruct((nodes, hidden_width), BF16), half, half),
+        out_shape=(jax.ShapeDtypeStruct((nodes, hidden_width), F32), half, half),
         in_specs=[vmem] * 5 + [smem],
         out_specs=(vmem, vmem, vmem),
         scratch_shapes=[pltpu.VMEM((ext, 2 * n_features), BF16)],
-        compiler_params=pltpu.CompilerParams(vmem_limit_bytes=24 * 2**20),
+        compiler_params=pltpu.CompilerParams(vmem_limit_bytes=12 * 2**20),
         cost_estimate=pl.CostEstimate(flops=600 * 10**6, bytes_accessed=4 * 10**6, transcendentals=nodes * hidden_width),
         name="layer",
     )(recv, adj, w_in, bias.reshape(1, hidden_width), cotangent, lax.axis_index("core").reshape(1))
 
-    pair = (mine + lax.ppermute(other, "core", [(0, 1), (1, 0)])).astype(BF16)
+    other = lax.ppermute(other, "core", [(0, 1), (1, 0)])
+    hidden, other = lax.optimization_barrier((hidden.astype(BF16), other))
+    pair = (mine + other).astype(BF16)
     copies = jnp.broadcast_to(pair[:, None], (chips, row_size, width, hidden_width))
     copies = copies.reshape(chips * row_size, width, hidden_width)
     pieces = lax.all_to_all(copies, ("x", "rows"), split_axis=0, concat_axis=0, tiled=True)

time: 50.5 us -> 49.7 us (0.984)
  waiting for transfers between devices: 10.5 us -> 9.62 us
  Pallas kernels: 5.43 us -> 4.64 us
  other arithmetic: 0.71 us -> 1.5 us
    pallas_call x1, Pallas kernels: 2.46 us -> 1.58 us  [body(): pl.pallas_call(layer_kernel, out_shape=(jax.ShapeDtypeStruct((nodes, hidd...]
    ppermute x1, waiting for transfers between devices: 1.25 us -> 0.45 us  [body(): other = lax.ppermute(other, 'core', [(0, 1), (1, 0)])]
    convert_element_type x1 -> x2, other arithmetic: 0.01 us -> 0.8 us  [the longest x1 0.79 us: body(): hidden, other = lax.optimization_barrier((hidden.astype(BF16), other))]
  transfers between devices with their start and end apart: 2 -> 2, of which waited for: 2 -> 2; matrix products, arithmetic and copies ran while one was open for 0% -> 2% of each run, Pallas kernels for 3% -> 3%
where the time goes in v4:
time: 49.7 us; the launch traced here: 49.4 us
  blocking collectives  18 us (36%)
  starting transfers between devices  11.2 us (23%)
  waiting for transfers between devices  9.62 us (19%)
  Pallas kernels  4.64 us (9%)
  local copies, waits for them, and re-layouts  3.71 us (7%)
  other arithmetic  1.5 us (3%)
  between operations  0.72 us (1%)
    all_to_all x1, blocking collectives, body(): lax.all_to_all(copies, ('x', 'rows'), split_axis=0, concat_axis=0, tiled=...  18 us
    all_to_all x1, starting transfers between devices, body(): recv = lax.all_to_all(send, ALL, split_axis=0, concat_axis=0, tiled=True)  11.1 us
    all_to_all x1, waiting for transfers between devices, body(): recv = lax.all_to_all(send, ALL, split_axis=0, concat_axis=0, tiled=True)  9.16 us
    unnamed x14, local copies, waits for them, and re-layouts  3.68 us
    pallas_call x1, Pallas kernels, body(): pl.pallas_call(lambda *refs: adjacency_kernel(*refs, cycle=cycle), out_sh...  1.66 us
    pallas_call x1, Pallas kernels, body(): pl.pallas_call(layer_kernel, out_shape=(jax.ShapeDtypeStruct((nodes, hidd...  1.58 us
    pallas_call x1, Pallas kernels, body(): pl.pallas_call(lambda *refs: send_kernel(*refs, ring=row_size), out_shape...  1.41 us
  transfers between devices with their start and end apart: 2, of which 2 were waited for; matrix products, arithmetic and copies ran while one was open for 2% of the time, Pallas kernels for 3%

profile of v4, /device:TPU:0, one launch (start us, length us, event | category | flops | bytes accessed | tf_op | source)
XLA Modules:
  0.0 49.4 jit_solution(17437625429753343241)
XLA Ops:
  0.6 0.0 copy-start.2
  0.6 0.9 %copy-done.2 = bf16[16,128,48]{1,2,0:T(8,128)(2,1)S(1)} copy-done((bf16[16,128,48]{1,2,0:T(8,128)(2,1)S(1)}, bf16[16,128,48]{1,2,0:T(8,128)(2,1)}, u32[]{:S(2)}) %copy-start.2) | copy-done | bytes 196632
  1.6 1.4 %pieces.1 = bf16[128,16,128]{2,1,0:T(8,128)(2,1)} custom-call(s32[1]{0:T(128)} %bitcast.refs_0_, bf16[16,48,128]{2,1,0:T(8,128)(2,1)S(1)} %bitcast.8), custom_call_target="tpu_custom_call" | custom-call | tf_op jit(solution)/shard_map/pieces/pallas_call | solution.py:123
  3.0 0.0 copy-start.1
  3.0 0.0 copy-start.3
  3.0 11.1 %all-to-all-start = ((bf16[128,16,128]{2,1,0:T(8,128)(2,1)}), bf16[128,16,128]{2,1,0:T(8,128)(2,1)S(1)}, u32[]{:S(2)}, u32[]{:S(2)}) async-start(bf16[128,16,128]{2,1,0:T(8,128)(2,1)} %pieces.1), calls=%async_computation | async-start | bytes 1048576 | tf_op jit(solution)/shard_map/all_to_all | solution.py:132
  14.1 0.0 copy-start.5
  14.1 0.0 copy-start
  14.2 1.4 %copy-done = bf16[6,8,128,128]{3,2,1,0:T(8,128)(2,1)S(1)} copy-done((bf16[6,8,128,128]{3,2,1,0:T(8,128)(2,1)S(1)}, bf16[6,8,128,128]{3,2,1,0:T(8,128)(2,1)}, u32[]{:S(2)}) %copy-start) | copy-done | bytes 1572888
  15.6 0.0 copy-start.4
  15.6 0.7 %copy-done.4 = s32[6,8]{1,0:T(8,128)S(1)} copy-done((s32[6,8]{1,0:T(8,128)S(1)}, s32[6,8]{1,0:T(8,128)}, u32[]{:S(2)}) %copy-start.4) | copy-done | bytes 216
  16.2 0.0 copy-start.6
  16.2 0.7 %copy-done.6 = s32[6]{0:T(128)S(1)} copy-done((s32[6]{0:T(128)S(1)}, s32[6]{0:T(128)}, u32[]{:S(2)}) %copy-start.6) | copy-done | bytes 48
  16.9 1.7 %adjacency.1.adj_ref = bf16[768,1280]{1,0:T(8,128)(2,1)S(1)} custom-call(s32[6,8]{1,0:T(8,128)S(1)} %copy-done.4, s32[6]{0:T(128)S(1)} %copy-done.6, s32[1]{0:T(128)} %bitcast.3.refs_2_, bf16[6,8,128,128]{3,2,1,0:T(8,128)(2,1)S(1)} %copy-done), custom_call_target="tpu_custom_call" | custom-call | flops 2000000 | bytes 4000000 | tf_op jit(solution)/shard_map/adjacency/pallas_call | solution.py:137
  18.6 9.2 %all-to-all-done = bf16[128,16,128]{2,1,0:T(8,128)(2,1)S(1)} async-done(((bf16[128,16,128]{2,1,0:T(8,128)(2,1)}), bf16[128,16,128]{2,1,0:T(8,128)(2,1)S(1)}, u32[]{:S(2)}, u32[]{:S(2)}) %all-to-all-start) | async-done | bytes 524320 | tf_op jit(solution)/shard_map/all_to_all | solution.py:132
  27.7 0.0 copy-done.1
  27.7 0.0 copy-done.3
  27.7 0.0 copy-done.5
  27.7 1.6 %layer.1 = (f32[768,256]{1,0:T(8,128)S(1)}, f32[4,16,256]{2,1,0:T(8,128)S(1)}, f32[4,16,256]{2,1,0:T(8,128)S(1)}) custom-call(bf16[8,16,16,128]{3,2,1,0:T(8,128)(2,1)S(1)} %bitcast.7, bf16[768,1280]{1,0:T(8,128)(2,1)S(1)} %adjacency.1.adj_ref, bf16[128,256]{1,0:T(8,128)(2,1)S(1)} %copy-done.3, f32[1,256]{1,0:T(1,128)S(1)} %bitcast.9, ...), custom_call_target="tpu_custom_call" | custom-call | flops 600000000 | bytes 4000000 | tf_op jit(solution)/shard_map/layer/pallas_call | solution.py:148
  29.3 0.1 collective-permute-start
  29.4 0.8 %convert_element_type.9 = bf16[768,256]{1,0:T(8,128)(2,1)} convert(f32[768,256]{1,0:T(8,128)S(1)} %get-tuple-element.7) | non-fusion elementwise | flops 196608 | bytes 1179648 | tf_op jit(solution)/shard_map/convert_element_type | solution.py:160
  30.2 0.5 collective-permute-done
  30.7 18.0 %all_to_all.10 = bf16[64,16,256]{2,1,0:T(8,128)(2,1)S(1)} all-to-all(bf16[64,16,256]{2,1,0:T(8,128)(2,1)S(1)} %bitcast.10), channel_id=1, replica_groups=mesh['x'=4,'core'=2,'rows'=16] {'x','rows'}, dimensions={0} | all-to-all | bytes 1048576 | tf_op jit(solution)/shard_map/all_to_all | solution.py:164
  48.7 0.7 %convert_reduce_fusion = f32[16,256]{1,0:T(8,128)} fusion(bf16[64,16,256]{2,1,0:T(8,128)(2,1)S(1)} %all_to_all.10), kind=kLoop, calls=%fused_computation | loop fusion | flops 520192 | bytes 540672 | tf_op jit(solution)/shard_map/reduce_sum | solution.py:165
  (2 shorter events, 0.0 us)
Async XLA Ops:
  0.6 0.9 %copy-start.2 = (bf16[16,128,48]{1,2,0:T(8,128)(2,1)S(1)}, bf16[16,128,48]{1,2,0:T(8,128)(2,1)}, u32[]{:S(2)}) copy-start(bf16[16,128,48]{1,2,0:T(8,128)(2,1)} %param.7) | copy-start | bytes 589828
  3.0 24.8 %copy-start.1 = (bf16[768,256]{1,0:T(8,128)(2,1)S(1)}, bf16[768,256]{1,0:T(8,128)(2,1)}, u32[]{:S(2)}) copy-start(bf16[768,256]{1,0:T(8,128)(2,1)} %cot_ref.1) | copy-start | bytes 1179652
  3.0 24.8 %copy-start.3 = (bf16[128,256]{1,0:T(8,128)(2,1)S(1)}, bf16[128,256]{1,0:T(8,128)(2,1)}, u32[]{:S(2)}) copy-start(bf16[128,256]{1,0:T(8,128)(2,1)} %w_ref.1) | copy-start | bytes 196612
  3.0 24.8 %all-to-all-start = ((bf16[128,16,128]{2,1,0:T(8,128)(2,1)}), bf16[128,16,128]{2,1,0:T(8,128)(2,1)S(1)}, u32[]{:S(2)}, u32[]{:S(2)}) async-start(bf16[128,16,128]{2,1,0:T(8,128)(2,1)} %pieces.1), calls=%async_computation | async-start | bytes 1048576 | tf_op jit(solution)/shard_map/all_to_all | solution.py:132
  14.1 13.6 %copy-start.5 = (f32[256]{0:T(256)S(1)}, f32[256]{0:T(256)}, u32[]{:S(2)}) copy-start(f32[256]{0:T(256)} %param.9) | copy-start | bytes 3076
  14.1 1.4 %copy-start = (bf16[6,8,128,128]{3,2,1,0:T(8,128)(2,1)S(1)}, bf16[6,8,128,128]{3,2,1,0:T(8,128)(2,1)}, u32[]{:S(2)}) copy-start(bf16[6,8,128,128]{3,2,1,0:T(8,128)(2,1)} %refs_3_.1) | copy-start | bytes 4718596
  15.6 0.7 %copy-start.4 = (s32[6,8]{1,0:T(8,128)S(1)}, s32[6,8]{1,0:T(8,128)}, u32[]{:S(2)}) copy-start(s32[6,8]{1,0:T(8,128)} %refs_0_.1) | copy-start | bytes 580
  16.2 0.7 %copy-start.6 = (s32[6]{0:T(128)S(1)}, s32[6]{0:T(128)}, u32[]{:S(2)}) copy-start(s32[6]{0:T(128)} %refs_1_.1) | copy-start | bytes 76
  29.3 1.3 %collective-permute-start = (f32[4,16,256]{2,1,0:T(8,128)S(1)}, f32[4,16,256]{2,1,0:T(8,128)S(1)}, u32[]{:S(2)}, u32[]{:S(2)}) collective-permute-start(f32[4,16,256]{2,1,0:T(8,128)S(1)} %get-tuple-element.8), channel_id=1, source_target_pairs={{0,16},{16,0},{1,17},{17,1},{2,18},{18,2},{3,19},{19,3},{4,20},{20... | collective-permute-start | bytes 196616 | tf_op jit(solution)/shard_map/ppermute | solution.py:159

commit v5 on v4

--- a/solution.py
+++ b/solution.py
@@ -8,6 +8,7 @@
 HALO_BLK = 2
 LANES = 128
 CORES = 2
+PARTS = 4
 FEAT = ("x", "core")
 ALL = ("x", "core", "rows")
 CHUNK = 768
@@ -16,7 +17,16 @@
 BF16 = jnp.bfloat16
 
 
-def adjacency_kernel(cols_ref, counts_ref, base_ref, tiles_ref, adj_ref, *, cycle):
+def adjacency_kernel(cols_ref, counts_ref, base_ref, tiles_ref, w_ref, adj_ref, ww_ref, *, cycle, slices):
+    features = w_ref.shape[0]
+    quarter = features // slices // PARTS
+    i = lax.broadcasted_iota(jnp.int32, (features, features), 0)
+    k = lax.broadcasted_iota(jnp.int32, (features, features), 1)
+    per = slices * quarter
+    source = (lax.rem(i, per) // quarter) * (PARTS * quarter) + (i // per) * quarter + lax.rem(i, quarter)
+    order = jnp.where(k == source, 1.0, 0.0).astype(BF16)
+    w = jnp.dot(order, w_ref[...], preferred_element_type=F32).astype(BF16)
+    ww_ref[...] = jnp.concatenate([w, w], axis=0)
     nb, slots, side, _ = tiles_ref.shape
     adj_ref[...] = jnp.zeros_like(adj_ref)
     eye = (
@@ -39,33 +49,46 @@
 
 def send_kernel(step_ref, x_ref, out_ref, rows_ref, *, ring):
     width, part, owners = x_ref.shape
+    quarter = width // PARTS
+    third = LANES - 2 * part
     i = lax.broadcasted_iota(jnp.int32, (owners, owners), 0)
     k = lax.broadcasted_iota(jnp.int32, (owners, owners), 1)
     beside = (i // ring) * ring + lax.rem(lax.rem(i, ring) + step_ref[0] + ring, ring)
     pick = jnp.concatenate([jnp.where(k == i, 1.0, 0.0), jnp.where(k == beside, 1.0, 0.0)], axis=1).astype(BF16)
     none = jnp.zeros((part, owners), BF16)
-    rest = jnp.zeros((LANES - 2 * part, 2 * owners), BF16)
-    for c in range(width):
+
+    def both(c):
         x = x_ref[c]
-        spread = jnp.concatenate(
-            [jnp.concatenate([x, none], axis=1), jnp.concatenate([none, x], axis=1), rest], axis=0
-        )
-        rows_ref[pl.ds(c, owners, stride=width), :] = lax.dot_general(
-            pick, spread, (((1,), (1,)), ((), ())), preferred_element_type=F32
-        )
-    out_ref[...] = rows_ref[...].astype(BF16).reshape(out_ref.shape)
-
-
-def layer_kernel(recv_ref, adj_ref, w_ref, bias_ref, cot_ref, core_ref, hidden_ref, mine_ref, other_ref, x_ref):
-    groups, senders, width, lanes = recv_ref.shape
-    features = groups * width
+        return jnp.concatenate([jnp.concatenate([x, none], axis=1), jnp.concatenate([none, x], axis=1)], axis=0)
+
+    count = owners * quarter
+    for b in range(quarter):
+        last = both((PARTS - 1) * quarter + b)
+        for t in range(PARTS - 1):
+            spread = jnp.concatenate([both(t * quarter + b), last[t * third : (t + 1) * third]], axis=0)
+            rows_ref[pl.ds(t * count + b, owners, stride=quarter), :] = lax.dot_general(
+                pick, spread, (((1,), (1,)), ((), ())), preferred_element_type=F32
+            )
+    for t in range(PARTS - 1):
+        rows = rows_ref[t * count : (t + 1) * count, :].astype(BF16)
+        out_ref[:, :, t * LANES : (t + 1) * LANES] = rows.reshape(owners, quarter, LANES)
+
+
+def layer_kernel(recv_ref, adj_ref, ww_ref, bias_ref, cot_ref, core_ref, hidden_ref, mine_ref, other_ref, x_ref):
+    groups, senders, quarter, _ = recv_ref.shape
+    per = groups * quarter
+    features = PARTS * per
     nodes = hidden_ref.shape[0]
     ext = x_ref.shape[0]
     halo = (ext - nodes) // 2
     part = nodes // senders
     x_ref[:, features:] = jnp.ones((ext, features), BF16)
     for r in range(senders):
-        piece = recv_ref[:, r].reshape(features, lanes).T
+        tiles = [
+            recv_ref[:, r, :, t * LANES : (t + 1) * LANES].reshape(per, LANES) for t in range(PARTS - 1)
+        ]
+        last = [tile[:, 2 * part :] for tile in tiles] + [jnp.zeros((per, LANES - 2 * part), BF16)]
+        piece = jnp.concatenate(tiles + [jnp.concatenate(last, axis=1)], axis=0).T
         x_ref[halo + r * part : halo + (r + 1) * part, :features] = piece[:part]
         first, last = r * part, (r + 1) * part
         if first < halo:
@@ -75,10 +98,9 @@
             skip = max(nodes - halo - first, 0)
             to = first + skip - (nodes - halo)
             x_ref[to : to + part - skip, :features] = piece[part + skip : 2 * part]
-    w = w_ref[...]
-    ww = jnp.concatenate([w, w], axis=0)
+    ww = ww_ref[...]
     bias = bias_ref[...]
-    hidden_width = w.shape[1]
+    hidden_width = ww.shape[1]
     total = jnp.zeros((2 * features, hidden_width), F32)
     for b in range(nodes // CHUNK):
         rows = pl.ds(b * CHUNK, CHUNK)
@@ -99,10 +121,13 @@
         scaled = (cot_ref[rows, :].astype(F32) * inv * slope).astype(BF16)
         total += lax.dot_general(yy, scaled, (((0,), (0,)), ((), ())), preferred_element_type=F32)
     total = total[:features] + total[features:]
-    total = total.reshape(mine_ref.shape[0], CORES, width, hidden_width)
     first = core_ref[0] == 0
-    mine_ref[...] = jnp.where(first, total[:, 0], total[:, 1])
-    other_ref[...] = jnp.where(first, total[:, 1], total[:, 0])
+    for chip in range(mine_ref.shape[0]):
+        at = [q * per + chip * CORES * quarter for q in range(PARTS)]
+        even = jnp.concatenate([total[i : i + quarter] for i in at], axis=0)
+        odd = jnp.concatenate([total[i + quarter : i + 2 * quarter] for i in at], axis=0)
+        mine_ref[chip] = jnp.where(first, even, odd)
+        other_ref[chip] = jnp.where(first, odd, even)
 
 
 def body(features, w_in, bias, tiles, tile_cols, tile_counts, cotangent):
@@ -122,27 +147,30 @@
     step = jnp.where(row_id * 2 < row_size, 1, -1).reshape(1).astype(jnp.int32)
     send = pl.pallas_call(
         lambda *refs: send_kernel(*refs, ring=row_size),
-        out_shape=jax.ShapeDtypeStruct((owners, width, LANES), BF16),
+        out_shape=jax.ShapeDtypeStruct((owners, width // PARTS, (PARTS - 1) * LANES), BF16),
         in_specs=[smem, vmem],
         out_specs=vmem,
-        scratch_shapes=[pltpu.VMEM((owners * width, LANES), F32)],
+        scratch_shapes=[pltpu.VMEM((owners * (width - width // PARTS), LANES), F32)],
         compiler_params=pltpu.CompilerParams(vmem_limit_bytes=4 * 2**20),
         name="pieces",
     )(step, features.transpose(0, 2, 1))
     recv = lax.all_to_all(send, ALL, split_axis=0, concat_axis=0, tiled=True)
-    recv = recv.reshape(feat_size, row_size, width, LANES)
+    recv = recv.reshape(feat_size, row_size, width // PARTS, (PARTS - 1) * LANES)
 
     base = (feat_id * cycle + row_id * block_rows).reshape(1).astype(jnp.int32)
     ext = nodes + 2 * halo
-    adj = pl.pallas_call(
-        lambda *refs: adjacency_kernel(*refs, cycle=cycle),
-        out_shape=jax.ShapeDtypeStruct((nodes, ext), BF16),
-        in_specs=[smem, smem, smem, vmem],
-        out_specs=vmem,
+    adj, ww = pl.pallas_call(
+        lambda *refs: adjacency_kernel(*refs, cycle=cycle, slices=feat_size),
+        out_shape=(
+            jax.ShapeDtypeStruct((nodes, ext), BF16),
+            jax.ShapeDtypeStruct((2 * n_features, hidden_width), BF16),
+        ),
+        in_specs=[smem, smem, smem, vmem, vmem],
+        out_specs=(vmem, vmem),
         compiler_params=pltpu.CompilerParams(vmem_limit_bytes=2 * 2**20),
         cost_estimate=pl.CostEstimate(flops=2 * 10**6, bytes_accessed=4 * 10**6, transcendentals=0),
         name="adjacency",
-    )(tile_cols, tile_counts, base, tiles)
+    )(tile_cols, tile_counts, base, tiles, w_in)
     chips = feat_size // CORES
     half = jax.ShapeDtypeStruct((chips, width, hidden_width), F32)
     hidden, mine, other = pl.pallas_call(
@@ -154,7 +182,7 @@
         compiler_params=pltpu.CompilerParams(vmem_limit_bytes=12 * 2**20),
         cost_estimate=pl.CostEstimate(flops=600 * 10**6, bytes_accessed=4 * 10**6, transcendentals=nodes * hidden_width),
         name="layer",
-    )(recv, adj, w_in, bias.reshape(1, hidden_width), cotangent, lax.axis_index("core").reshape(1))
+    )(recv, adj, ww, bias.reshape(1, hidden_width), cotangent, lax.axis_index("core").reshape(1))
 
     other = lax.ppermute(other, "core", [(0, 1), (1, 0)])
     hidden, other = lax.optimization_barrier((hidden.astype(BF16), other))

time: 49.7 us -> 48.4 us (0.974)
  waiting for transfers between devices: 9.62 us -> 7.24 us
  local copies, waits for them, and re-layouts: 3.71 us -> 4.59 us
    all_to_all x1, waiting for transfers between devices: 9.16 us -> 6.79 us  [body(): recv = lax.all_to_all(send, ALL, split_axis=0, concat_axis=0, tiled=True)]
    unnamed x14, local copies, waits for them, and re-layouts: 3.68 us -> 4.56 us
  transfers between devices with their start and end apart: 2 -> 2, of which waited for: 2 -> 2; matrix products, arithmetic and copies ran while one was open for 2% -> 2% of each run, Pallas kernels for 3% -> 4%
where the time goes in v5:
time: 48.4 us; the launch traced here: 48.1 us
  blocking collectives  18.1 us (37%)
  starting transfers between devices  11.2 us (23%)
  waiting for transfers between devices  7.24 us (15%)
  Pallas kernels  4.72 us (10%)
  local copies, waits for them, and re-layouts  4.59 us (9%)
  other arithmetic  1.5 us (3%)
  between operations  0.72 us (1%)
    all_to_all x1, blocking collectives, body(): lax.all_to_all(copies, ('x', 'rows'), split_axis=0, concat_axis=0, tiled=...  18.1 us
    all_to_all x1, starting transfers between devices, body(): recv = lax.all_to_all(send, ALL, split_axis=0, concat_axis=0, tiled=True)  11.1 us
    all_to_all x1, waiting for transfers between devices, body(): recv = lax.all_to_all(send, ALL, split_axis=0, concat_axis=0, tiled=True)  6.79 us
    unnamed x14, local copies, waits for them, and re-layouts  4.56 us
    pallas_call x1, Pallas kernels, body(): pl.pallas_call(lambda *refs: adjacency_kernel(*refs, cycle=cycle, slices=...  1.85 us
    pallas_call x1, Pallas kernels, body(): pl.pallas_call(layer_kernel, out_shape=(jax.ShapeDtypeStruct((nodes, hidd...  1.68 us
    pallas_call x1, Pallas kernels, body(): pl.pallas_call(lambda *refs: send_kernel(*refs, ring=row_size), out_shape...  1.19 us
  transfers between devices with their start and end apart: 2, of which 2 were waited for; matrix products, arithmetic and copies ran while one was open for 2% of the time, Pallas kernels for 4%

profile of v5, /device:TPU:0, one launch (start us, length us, event | category | flops | bytes accessed | tf_op | source)
XLA Modules:
  0.0 48.1 jit_solution(12872147882977111320)
XLA Ops:
  0.6 0.0 copy-start.1
  0.6 0.0 copy-start.2
  0.7 1.0 %copy-done.2 = bf16[16,128,48]{1,2,0:T(8,128)(2,1)S(1)} copy-done((bf16[16,128,48]{1,2,0:T(8,128)(2,1)S(1)}, bf16[16,128,48]{1,2,0:T(8,128)(2,1)}, u32[]{:S(2)}) %copy-start.2) | copy-done | bytes 196632
  1.6 0.0 copy-start.5
  1.6 1.2 %pieces.1 = bf16[128,4,384]{2,1,0:T(4,128)(2,1)} custom-call(s32[1]{0:T(128)} %bitcast.refs_0_, bf16[16,48,128]{2,1,0:T(8,128)(2,1)S(1)} %bitcast.8), custom_call_target="tpu_custom_call" | custom-call | tf_op jit(solution)/shard_map/pieces/pallas_call | solution.py:148
  2.8 11.1 %all-to-all-start = ((bf16[128,4,384]{2,1,0:T(4,128)(2,1)}), bf16[128,4,384]{2,1,0:T(4,128)(2,1)S(1)}, u32[]{:S(2)}, u32[]{:S(2)}) async-start(bf16[128,4,384]{2,1,0:T(4,128)(2,1)} %pieces.1), calls=%async_computation | async-start | bytes 786432 | tf_op jit(solution)/shard_map/all_to_all | solution.py:157
  14.0 0.0 copy-start
  14.0 1.4 %copy-done = bf16[6,8,128,128]{3,2,1,0:T(8,128)(2,1)S(1)} copy-done((bf16[6,8,128,128]{3,2,1,0:T(8,128)(2,1)S(1)}, bf16[6,8,128,128]{3,2,1,0:T(8,128)(2,1)}, u32[]{:S(2)}) %copy-start) | copy-done | bytes 1572888
  15.4 0.0 copy-start.3
  15.4 0.8 %copy-done.3 = bf16[128,256]{1,0:T(8,128)(2,1)S(1)} copy-done((bf16[128,256]{1,0:T(8,128)(2,1)S(1)}, bf16[128,256]{1,0:T(8,128)(2,1)}, u32[]{:S(2)}) %copy-start.3) | copy-done | bytes 65560
  16.2 0.0 copy-start.4
  16.2 0.7 %copy-done.4 = s32[6,8]{1,0:T(8,128)S(1)} copy-done((s32[6,8]{1,0:T(8,128)S(1)}, s32[6,8]{1,0:T(8,128)}, u32[]{:S(2)}) %copy-start.4) | copy-done | bytes 216
  16.9 0.0 copy-start.6
  16.9 0.7 %copy-done.6 = s32[6]{0:T(128)S(1)} copy-done((s32[6]{0:T(128)S(1)}, s32[6]{0:T(128)}, u32[]{:S(2)}) %copy-start.6) | copy-done | bytes 48
  17.6 1.8 %adjacency.1 = (bf16[768,1280]{1,0:T(8,128)(2,1)S(1)}, bf16[256,256]{1,0:T(8,128)(2,1)S(1)}) custom-call(s32[6,8]{1,0:T(8,128)S(1)} %copy-done.4, s32[6]{0:T(128)S(1)} %copy-done.6, s32[1]{0:T(128)} %bitcast.3.refs_2_, bf16[6,8,128,128]{3,2,1,0:T(8,128)(2,1)S(1)} %copy-done, bf16[128,256]{1,0:T(8,128)(2,1)S(1)} %copy-done.3), custom_call_target="tpu_custom_call" | custom-call | flops 2000000 | bytes 4000000 | tf_op jit(solution)/shard_map/adjacency/pallas_call | solution.py:162
  19.4 6.8 %all-to-all-done = bf16[128,4,384]{2,1,0:T(4,128)(2,1)S(1)} async-done(((bf16[128,4,384]{2,1,0:T(4,128)(2,1)}), bf16[128,4,384]{2,1,0:T(4,128)(2,1)S(1)}, u32[]{:S(2)}, u32[]{:S(2)}) %all-to-all-start) | async-done | bytes 393248 | tf_op jit(solution)/shard_map/all_to_all | solution.py:157
  26.2 0.0 copy-done.1
  26.2 0.0 copy-done.5
  26.2 1.7 %layer.1 = (f32[768,256]{1,0:T(8,128)S(1)}, f32[4,16,256]{2,1,0:T(8,128)S(1)}, f32[4,16,256]{2,1,0:T(8,128)S(1)}) custom-call(bf16[8,16,4,384]{3,2,1,0:T(4,128)(2,1)S(1)} %bitcast.7, bf16[768,1280]{1,0:T(8,128)(2,1)S(1)} %get-tuple-element.9.adj_ref, bf16[256,256]{1,0:T(8,128)(2,1)S(1)} %get-tuple-element.10.ww_ref, f32[1,256]{1,0:T(1,128)S(1)} %bitcast.9, ...), custom_call_target="tpu_custom_call" | custom-call | flops 600000000 | bytes 4000000 | tf_op jit(solution)/shard_map/layer/pallas_call | solution.py:176
  27.9 0.1 collective-permute-start
  28.0 0.8 %convert_element_type.9 = bf16[768,256]{1,0:T(8,128)(2,1)} convert(f32[768,256]{1,0:T(8,128)S(1)} %get-tuple-element.11) | non-fusion elementwise | flops 196608 | bytes 1179648 | tf_op jit(solution)/shard_map/convert_element_type | solution.py:188
  28.8 0.5 collective-permute-done
  29.3 18.1 %all_to_all.10 = bf16[64,16,256]{2,1,0:T(8,128)(2,1)S(1)} all-to-all(bf16[64,16,256]{2,1,0:T(8,128)(2,1)S(1)} %bitcast.10), channel_id=1, replica_groups=mesh['x'=4,'core'=2,'rows'=16] {'x','rows'}, dimensions={0} | all-to-all | bytes 1048576 | tf_op jit(solution)/shard_map/all_to_all | solution.py:192
  47.4 0.7 %convert_reduce_fusion = f32[16,256]{1,0:T(8,128)} fusion(bf16[64,16,256]{2,1,0:T(8,128)(2,1)S(1)} %all_to_all.10), kind=kLoop, calls=%fused_computation | loop fusion | flops 520192 | bytes 540672 | tf_op jit(solution)/shard_map/reduce_sum | solution.py:193
  (2 shorter events, 0.0 us)
Async XLA Ops:
  0.6 25.6 %copy-start.1 = (bf16[768,256]{1,0:T(8,128)(2,1)S(1)}, bf16[768,256]{1,0:T(8,128)(2,1)}, u32[]{:S(2)}) copy-start(bf16[768,256]{1,0:T(8,128)(2,1)} %cot_ref.1) | copy-start | bytes 1179652
  0.6 1.0 %copy-start.2 = (bf16[16,128,48]{1,2,0:T(8,128)(2,1)S(1)}, bf16[16,128,48]{1,2,0:T(8,128)(2,1)}, u32[]{:S(2)}) copy-start(bf16[16,128,48]{1,2,0:T(8,128)(2,1)} %param.7) | copy-start | bytes 589828
  1.6 24.6 %copy-start.5 = (f32[256]{0:T(256)S(1)}, f32[256]{0:T(256)}, u32[]{:S(2)}) copy-start(f32[256]{0:T(256)} %param.9) | copy-start | bytes 3076
  2.8 23.4 %all-to-all-start = ((bf16[128,4,384]{2,1,0:T(4,128)(2,1)}), bf16[128,4,384]{2,1,0:T(4,128)(2,1)S(1)}, u32[]{:S(2)}, u32[]{:S(2)}) async-start(bf16[128,4,384]{2,1,0:T(4,128)(2,1)} %pieces.1), calls=%async_computation | async-start | bytes 786432 | tf_op jit(solution)/shard_map/all_to_all | solution.py:157
  14.0 1.4 %copy-start = (bf16[6,8,128,128]{3,2,1,0:T(8,128)(2,1)S(1)}, bf16[6,8,128,128]{3,2,1,0:T(8,128)(2,1)}, u32[]{:S(2)}) copy-start(bf16[6,8,128,128]{3,2,1,0:T(8,128)(2,1)} %refs_3_.1) | copy-start | bytes 4718596
  15.4 0.8 %copy-start.3 = (bf16[128,256]{1,0:T(8,128)(2,1)S(1)}, bf16[128,256]{1,0:T(8,128)(2,1)}, u32[]{:S(2)}) copy-start(bf16[128,256]{1,0:T(8,128)(2,1)} %refs_4_.1) | copy-start | bytes 196612
  16.2 0.7 %copy-start.4 = (s32[6,8]{1,0:T(8,128)S(1)}, s32[6,8]{1,0:T(8,128)}, u32[]{:S(2)}) copy-start(s32[6,8]{1,0:T(8,128)} %refs_0_.1) | copy-start | bytes 580
  16.9 0.7 %copy-start.6 = (s32[6]{0:T(128)S(1)}, s32[6]{0:T(128)}, u32[]{:S(2)}) copy-start(s32[6]{0:T(128)} %refs_1_.1) | copy-start | bytes 76
  27.9 1.3 %collective-permute-start = (f32[4,16,256]{2,1,0:T(8,128)S(1)}, f32[4,16,256]{2,1,0:T(8,128)S(1)}, u32[]{:S(2)}, u32[]{:S(2)}) collective-permute-start(f32[4,16,256]{2,1,0:T(8,128)S(1)} %get-tuple-element.12), channel_id=1, source_target_pairs={{0,16},{16,0},{1,17},{17,1},{2,18},{18,2},{3,19},{19,3},{4,20},{20... | collective-permute-start | bytes 196616 | tf_op jit(solution)/shard_map/ppermute | solution.py:187

commit v6 on v5

--- a/solution.py
+++ b/solution.py
@@ -9,6 +9,7 @@
 LANES = 128
 CORES = 2
 PARTS = 4
+COPIES = 2
 FEAT = ("x", "core")
 ALL = ("x", "core", "rows")
 CHUNK = 768
@@ -47,15 +48,22 @@
                 adj_ref[at] = adj_ref[at] + tiles_ref[b, k]
 
 
-def send_kernel(step_ref, x_ref, out_ref, rows_ref, *, ring):
+def send_kernel(step_ref, x_hbm, out_hbm, x_ref, rows_ref, out_ref, load_sem, store_sem, *, ring):
     width, part, owners = x_ref.shape
     quarter = width // PARTS
     third = LANES - 2 * part
+    loads = []
+    for n in range(COPIES):
+        at = pl.ds(n * (width // COPIES), width // COPIES)
+        loads.append(pltpu.make_async_copy(x_hbm.at[at], x_ref.at[at], load_sem.at[n]))
+        loads[n].start()
     i = lax.broadcasted_iota(jnp.int32, (owners, owners), 0)
     k = lax.broadcasted_iota(jnp.int32, (owners, owners), 1)
     beside = (i // ring) * ring + lax.rem(lax.rem(i, ring) + step_ref[0] + ring, ring)
     pick = jnp.concatenate([jnp.where(k == i, 1.0, 0.0), jnp.where(k == beside, 1.0, 0.0)], axis=1).astype(BF16)
     none = jnp.zeros((part, owners), BF16)
+    for load in loads:
+        load.wait()
 
     def both(c):
         x = x_ref[c]
@@ -69,9 +77,17 @@
             rows_ref[pl.ds(t * count + b, owners, stride=quarter), :] = lax.dot_general(
                 pick, spread, (((1,), (1,)), ((), ())), preferred_element_type=F32
             )
-    for t in range(PARTS - 1):
-        rows = rows_ref[t * count : (t + 1) * count, :].astype(BF16)
-        out_ref[:, :, t * LANES : (t + 1) * LANES] = rows.reshape(owners, quarter, LANES)
+    stores = []
+    some = owners // COPIES
+    for n in range(COPIES):
+        at = pl.ds(n * some, some)
+        for t in range(PARTS - 1):
+            rows = rows_ref[pl.ds(t * count + n * some * quarter, some * quarter), :].astype(BF16)
+            out_ref[at, :, t * LANES : (t + 1) * LANES] = rows.reshape(some, quarter, LANES)
+        stores.append(pltpu.make_async_copy(out_ref.at[at], out_hbm.at[at], store_sem.at[n]))
+        stores[n].start()
+    for store in stores:
+        store.wait()
 
 
 def layer_kernel(recv_ref, adj_ref, ww_ref, bias_ref, cot_ref, core_ref, hidden_ref, mine_ref, other_ref, x_ref):
@@ -145,15 +161,23 @@
     vmem = pl.BlockSpec(memory_space=pltpu.VMEM)
     smem = pl.BlockSpec(memory_space=pltpu.SMEM)
     step = jnp.where(row_id * 2 < row_size, 1, -1).reshape(1).astype(jnp.int32)
+    hbm = pl.BlockSpec(memory_space=pltpu.MemorySpace.HBM)
+    sent = (owners, width // PARTS, (PARTS - 1) * LANES)
     send = pl.pallas_call(
         lambda *refs: send_kernel(*refs, ring=row_size),
-        out_shape=jax.ShapeDtypeStruct((owners, width // PARTS, (PARTS - 1) * LANES), BF16),
-        in_specs=[smem, vmem],
-        out_specs=vmem,
-        scratch_shapes=[pltpu.VMEM((owners * (width - width // PARTS), LANES), F32)],
+        out_shape=jax.ShapeDtypeStruct(sent, BF16),
+        in_specs=[smem, hbm],
+        out_specs=hbm,
+        scratch_shapes=[
+            pltpu.VMEM((width, part, owners), BF16),
+            pltpu.VMEM((owners * (width - width // PARTS), LANES), F32),
+            pltpu.VMEM(sent, BF16),
+            pltpu.SemaphoreType.DMA((COPIES,)),
+            pltpu.SemaphoreType.DMA((COPIES,)),
+        ],
         compiler_params=pltpu.CompilerParams(vmem_limit_bytes=4 * 2**20),
         name="pieces",
-    )(step, features.transpose(0, 2, 1))
+    )(step, pltpu.with_memory_space_constraint(features.transpose(0, 2, 1), pltpu.MemorySpace.HBM))
     recv = lax.all_to_all(send, ALL, split_axis=0, concat_axis=0, tiled=True)
     recv = recv.reshape(feat_size, row_size, width // PARTS, (PARTS - 1) * LANES)
 

time: 48.4 us -> 48.4 us (level)
  Pallas kernels: 4.72 us -> 5.72 us
  local copies, waits for them, and re-layouts: 4.59 us -> 3.63 us
    pallas_call x1, Pallas kernels: 1.19 us -> 2.17 us  [body(): pl.pallas_call(lambda *refs: send_kernel(*refs, ring=row_size), out_shape...]
    unnamed x14 -> x12, local copies, waits for them, and re-layouts: 4.56 us -> 3.59 us
where the time goes in v6:
time: 48.4 us; the launch traced here: 48.1 us
  blocking collectives  18.1 us (37%)
  starting transfers between devices  11.2 us (23%)
  waiting for transfers between devices  7.21 us (15%)
  Pallas kernels  5.72 us (12%)
  local copies, waits for them, and re-layouts  3.63 us (8%)
  other arithmetic  1.5 us (3%)
  between operations  0.73 us (2%)
    all_to_all x1, blocking collectives, body(): lax.all_to_all(copies, ('x', 'rows'), split_axis=0, concat_axis=0, tiled=...  18.1 us
    all_to_all x1, starting transfers between devices, body(): recv = lax.all_to_all(send, ALL, split_axis=0, concat_axis=0, tiled=True)  11.1 us
    all_to_all x1, waiting for transfers between devices, body(): recv = lax.all_to_all(send, ALL, split_axis=0, concat_axis=0, tiled=True)  6.76 us
    unnamed x12, local copies, waits for them, and re-layouts  3.59 us
    pallas_call x1, Pallas kernels, body(): pl.pallas_call(lambda *refs: send_kernel(*refs, ring=row_size), out_shape...  2.17 us
    pallas_call x1, Pallas kernels, body(): pl.pallas_call(lambda *refs: adjacency_kernel(*refs, cycle=cycle, slices=...  1.88 us
    pallas_call x1, Pallas kernels, body(): pl.pallas_call(layer_kernel, out_shape=(jax.ShapeDtypeStruct((nodes, hidd...  1.68 us
  transfers between devices with their start and end apart: 2, of which 2 were waited for; matrix products, arithmetic and copies ran while one was open for 2% of the time, Pallas kernels for 4%

profile of v6, /device:TPU:0, one launch (start us, length us, event | category | flops | bytes accessed | tf_op | source)
XLA Modules:
  0.0 48.1 jit_solution(3906282495314493782)
XLA Ops:
  0.6 0.0 copy-start.1
  0.6 0.0 copy-start.4
  0.7 2.2 %pieces.1 = bf16[128,4,384]{2,1,0:T(4,128)(2,1)} custom-call(s32[1]{0:T(128)} %bitcast.refs_0_, bf16[16,48,128]{2,1,0:T(8,128)(2,1)} %bitcast.10), custom_call_target="tpu_custom_call" | custom-call | tf_op jit(solution)/shard_map/pieces/pallas_call | solution.py:166
  2.8 11.1 %all-to-all-start = ((bf16[128,4,384]{2,1,0:T(4,128)(2,1)}), bf16[128,4,384]{2,1,0:T(4,128)(2,1)S(1)}, u32[]{:S(2)}, u32[]{:S(2)}) async-start(bf16[128,4,384]{2,1,0:T(4,128)(2,1)} %pieces.1), calls=%async_computation | async-start | bytes 786432 | tf_op jit(solution)/shard_map/all_to_all | solution.py:181
  14.0 0.0 copy-start
  14.0 1.4 %copy-done = bf16[6,8,128,128]{3,2,1,0:T(8,128)(2,1)S(1)} copy-done((bf16[6,8,128,128]{3,2,1,0:T(8,128)(2,1)S(1)}, bf16[6,8,128,128]{3,2,1,0:T(8,128)(2,1)}, u32[]{:S(2)}) %copy-start) | copy-done | bytes 1572888
  15.4 0.0 copy-start.2
  15.4 0.8 %copy-done.2 = bf16[128,256]{1,0:T(8,128)(2,1)S(1)} copy-done((bf16[128,256]{1,0:T(8,128)(2,1)S(1)}, bf16[128,256]{1,0:T(8,128)(2,1)}, u32[]{:S(2)}) %copy-start.2) | copy-done | bytes 65560
  16.3 0.0 copy-start.3
  16.3 0.7 %copy-done.3 = s32[6,8]{1,0:T(8,128)S(1)} copy-done((s32[6,8]{1,0:T(8,128)S(1)}, s32[6,8]{1,0:T(8,128)}, u32[]{:S(2)}) %copy-start.3) | copy-done | bytes 216
  16.9 0.0 copy-start.5
  16.9 0.7 %copy-done.5 = s32[6]{0:T(128)S(1)} copy-done((s32[6]{0:T(128)S(1)}, s32[6]{0:T(128)}, u32[]{:S(2)}) %copy-start.5) | copy-done | bytes 48
  17.6 1.9 %adjacency.1 = (bf16[768,1280]{1,0:T(8,128)(2,1)S(1)}, bf16[256,256]{1,0:T(8,128)(2,1)S(1)}) custom-call(s32[6,8]{1,0:T(8,128)S(1)} %copy-done.3, s32[6]{0:T(128)S(1)} %copy-done.5, s32[1]{0:T(128)} %bitcast.3.refs_2_, bf16[6,8,128,128]{3,2,1,0:T(8,128)(2,1)S(1)} %copy-done, bf16[128,256]{1,0:T(8,128)(2,1)S(1)} %copy-done.2), custom_call_target="tpu_custom_call" | custom-call | flops 2000000 | bytes 4000000 | tf_op jit(solution)/shard_map/adjacency/pallas_call | solution.py:186
  19.5 6.8 %all-to-all-done = bf16[128,4,384]{2,1,0:T(4,128)(2,1)S(1)} async-done(((bf16[128,4,384]{2,1,0:T(4,128)(2,1)}), bf16[128,4,384]{2,1,0:T(4,128)(2,1)S(1)}, u32[]{:S(2)}, u32[]{:S(2)}) %all-to-all-start) | async-done | bytes 393248 | tf_op jit(solution)/shard_map/all_to_all | solution.py:181
  26.2 0.0 copy-done.1
  26.2 0.0 copy-done.4
  26.2 1.7 %layer.1 = (f32[768,256]{1,0:T(8,128)S(1)}, f32[4,16,256]{2,1,0:T(8,128)S(1)}, f32[4,16,256]{2,1,0:T(8,128)S(1)}) custom-call(bf16[8,16,4,384]{3,2,1,0:T(4,128)(2,1)S(1)} %bitcast.7, bf16[768,1280]{1,0:T(8,128)(2,1)S(1)} %get-tuple-element.9.adj_ref, bf16[256,256]{1,0:T(8,128)(2,1)S(1)} %get-tuple-element.10.ww_ref, f32[1,256]{1,0:T(1,128)S(1)} %bitcast.8, ...), custom_call_target="tpu_custom_call" | custom-call | flops 600000000 | bytes 4000000 | tf_op jit(solution)/shard_map/layer/pallas_call | solution.py:200
  27.9 0.1 collective-permute-start
  28.0 0.8 %convert_element_type.9 = bf16[768,256]{1,0:T(8,128)(2,1)} convert(f32[768,256]{1,0:T(8,128)S(1)} %get-tuple-element.11) | non-fusion elementwise | flops 196608 | bytes 1179648 | tf_op jit(solution)/shard_map/convert_element_type | solution.py:212
  28.8 0.5 collective-permute-done
  29.3 18.1 %all_to_all.10 = bf16[64,16,256]{2,1,0:T(8,128)(2,1)S(1)} all-to-all(bf16[64,16,256]{2,1,0:T(8,128)(2,1)S(1)} %bitcast.9), channel_id=1, replica_groups=mesh['x'=4,'core'=2,'rows'=16] {'x','rows'}, dimensions={0} | all-to-all | bytes 1048576 | tf_op jit(solution)/shard_map/all_to_all | solution.py:216
  47.4 0.7 %convert_reduce_fusion = f32[16,256]{1,0:T(8,128)} fusion(bf16[64,16,256]{2,1,0:T(8,128)(2,1)S(1)} %all_to_all.10), kind=kLoop, calls=%fused_computation | loop fusion | flops 520192 | bytes 540672 | tf_op jit(solution)/shard_map/reduce_sum | solution.py:217
  (2 shorter events, 0.0 us)
Async XLA Ops:
  0.6 25.6 %copy-start.1 = (bf16[768,256]{1,0:T(8,128)(2,1)S(1)}, bf16[768,256]{1,0:T(8,128)(2,1)}, u32[]{:S(2)}) copy-start(bf16[768,256]{1,0:T(8,128)(2,1)} %cot_ref.1) | copy-start | bytes 1179652
  0.6 25.6 %copy-start.4 = (f32[256]{0:T(256)S(1)}, f32[256]{0:T(256)}, u32[]{:S(2)}) copy-start(f32[256]{0:T(256)} %param.9) | copy-start | bytes 3076
  2.8 23.4 %all-to-all-start = ((bf16[128,4,384]{2,1,0:T(4,128)(2,1)}), bf16[128,4,384]{2,1,0:T(4,128)(2,1)S(1)}, u32[]{:S(2)}, u32[]{:S(2)}) async-start(bf16[128,4,384]{2,1,0:T(4,128)(2,1)} %pieces.1), calls=%async_computation | async-start | bytes 786432 | tf_op jit(solution)/shard_map/all_to_all | solution.py:181
  14.0 1.4 %copy-start = (bf16[6,8,128,128]{3,2,1,0:T(8,128)(2,1)S(1)}, bf16[6,8,128,128]{3,2,1,0:T(8,128)(2,1)}, u32[]{:S(2)}) copy-start(bf16[6,8,128,128]{3,2,1,0:T(8,128)(2,1)} %refs_3_.1) | copy-start | bytes 4718596
  15.4 0.8 %copy-start.2 = (bf16[128,256]{1,0:T(8,128)(2,1)S(1)}, bf16[128,256]{1,0:T(8,128)(2,1)}, u32[]{:S(2)}) copy-start(bf16[128,256]{1,0:T(8,128)(2,1)} %refs_4_.1) | copy-start | bytes 196612
  16.3 0.7 %copy-start.3 = (s32[6,8]{1,0:T(8,128)S(1)}, s32[6,8]{1,0:T(8,128)}, u32[]{:S(2)}) copy-start(s32[6,8]{1,0:T(8,128)} %refs_0_.1) | copy-start | bytes 580
  16.9 0.7 %copy-start.5 = (s32[6]{0:T(128)S(1)}, s32[6]{0:T(128)}, u32[]{:S(2)}) copy-start(s32[6]{0:T(128)} %refs_1_.1) | copy-start | bytes 76
  27.9 1.3 %collective-permute-start = (f32[4,16,256]{2,1,0:T(8,128)S(1)}, f32[4,16,256]{2,1,0:T(8,128)S(1)}, u32[]{:S(2)}, u32[]{:S(2)}) collective-permute-start(f32[4,16,256]{2,1,0:T(8,128)S(1)} %get-tuple-element.12), channel_id=1, source_target_pairs={{0,16},{16,0},{1,17},{17,1},{2,18},{18,2},{3,19},{19,3},{4,20},{20... | collective-permute-start | bytes 196616 | tf_op jit(solution)/shard_map/ppermute | solution.py:211

commit v7 on v5

--- a/solution.py
+++ b/solution.py
@@ -17,16 +17,7 @@
 BF16 = jnp.bfloat16
 
 
-def adjacency_kernel(cols_ref, counts_ref, base_ref, tiles_ref, w_ref, adj_ref, ww_ref, *, cycle, slices):
-    features = w_ref.shape[0]
-    quarter = features // slices // PARTS
-    i = lax.broadcasted_iota(jnp.int32, (features, features), 0)
-    k = lax.broadcasted_iota(jnp.int32, (features, features), 1)
-    per = slices * quarter
-    source = (lax.rem(i, per) // quarter) * (PARTS * quarter) + (i // per) * quarter + lax.rem(i, quarter)
-    order = jnp.where(k == source, 1.0, 0.0).astype(BF16)
-    w = jnp.dot(order, w_ref[...], preferred_element_type=F32).astype(BF16)
-    ww_ref[...] = jnp.concatenate([w, w], axis=0)
+def adjacency_kernel(cols_ref, counts_ref, base_ref, tiles_ref, adj_ref, *, cycle):
     nb, slots, side, _ = tiles_ref.shape
     adj_ref[...] = jnp.zeros_like(adj_ref)
     eye = (
@@ -74,7 +65,9 @@
         out_ref[:, :, t * LANES : (t + 1) * LANES] = rows.reshape(owners, quarter, LANES)
 
 
-def layer_kernel(recv_ref, adj_ref, ww_ref, bias_ref, cot_ref, core_ref, hidden_ref, mine_ref, other_ref, x_ref):
+def layer_kernel(
+    recv_ref, adj_ref, w_hbm, bias_ref, cot_ref, core_ref, hidden_ref, mine_ref, other_ref, x_ref, w_ref, load_sem
+):
     groups, senders, quarter, _ = recv_ref.shape
     per = groups * quarter
     features = PARTS * per
@@ -82,6 +75,8 @@
     ext = x_ref.shape[0]
     halo = (ext - nodes) // 2
     part = nodes // senders
+    load = pltpu.make_async_copy(w_hbm, w_ref, load_sem)
+    load.start()
     x_ref[:, features:] = jnp.ones((ext, features), BF16)
     for r in range(senders):
         tiles = [
@@ -98,7 +93,13 @@
             skip = max(nodes - halo - first, 0)
             to = first + skip - (nodes - halo)
             x_ref[to : to + part - skip, :features] = piece[part + skip : 2 * part]
-    ww = ww_ref[...]
+    i = lax.broadcasted_iota(jnp.int32, (features, features), 0)
+    k = lax.broadcasted_iota(jnp.int32, (features, features), 1)
+    source = (lax.rem(i, per) // quarter) * (PARTS * quarter) + (i // per) * quarter + lax.rem(i, quarter)
+    order = jnp.where(k == source, 1.0, 0.0).astype(BF16)
+    load.wait()
+    w = jnp.dot(order, w_ref[...], preferred_element_type=F32).astype(BF16)
+    ww = jnp.concatenate([w, w], axis=0)
     bias = bias_ref[...]
     hidden_width = ww.shape[1]
     total = jnp.zeros((2 * features, hidden_width), F32)
@@ -151,7 +152,7 @@
         in_specs=[smem, vmem],
         out_specs=vmem,
         scratch_shapes=[pltpu.VMEM((owners * (width - width // PARTS), LANES), F32)],
-        compiler_params=pltpu.CompilerParams(vmem_limit_bytes=4 * 2**20),
+        compiler_params=pltpu.CompilerParams(vmem_limit_bytes=3 * 2**20),
         name="pieces",
     )(step, features.transpose(0, 2, 1))
     recv = lax.all_to_all(send, ALL, split_axis=0, concat_axis=0, tiled=True)
@@ -159,38 +160,38 @@
 
     base = (feat_id * cycle + row_id * block_rows).reshape(1).astype(jnp.int32)
     ext = nodes + 2 * halo
-    adj, ww = pl.pallas_call(
-        lambda *refs: adjacency_kernel(*refs, cycle=cycle, slices=feat_size),
-        out_shape=(
-            jax.ShapeDtypeStruct((nodes, ext), BF16),
-            jax.ShapeDtypeStruct((2 * n_features, hidden_width), BF16),
-        ),
-        in_specs=[smem, smem, smem, vmem, vmem],
-        out_specs=(vmem, vmem),
+    adj = pl.pallas_call(
+        lambda *refs: adjacency_kernel(*refs, cycle=cycle),
+        out_shape=jax.ShapeDtypeStruct((nodes, ext), BF16),
+        in_specs=[smem, smem, smem, vmem],
+        out_specs=vmem,
         compiler_params=pltpu.CompilerParams(vmem_limit_bytes=2 * 2**20),
         cost_estimate=pl.CostEstimate(flops=2 * 10**6, bytes_accessed=4 * 10**6, transcendentals=0),
         name="adjacency",
-    )(tile_cols, tile_counts, base, tiles, w_in)
+    )(tile_cols, tile_counts, base, tiles)
     chips = feat_size // CORES
     half = jax.ShapeDtypeStruct((chips, width, hidden_width), F32)
     hidden, mine, other = pl.pallas_call(
         layer_kernel,
         out_shape=(jax.ShapeDtypeStruct((nodes, hidden_width), F32), half, half),
-        in_specs=[vmem] * 5 + [smem],
+        in_specs=[vmem, vmem, pl.BlockSpec(memory_space=pltpu.MemorySpace.HBM), vmem, vmem, smem],
         out_specs=(vmem, vmem, vmem),
-        scratch_shapes=[pltpu.VMEM((ext, 2 * n_features), BF16)],
-        compiler_params=pltpu.CompilerParams(vmem_limit_bytes=12 * 2**20),
+        scratch_shapes=[
+            pltpu.VMEM((ext, 2 * n_features), BF16),
+            pltpu.VMEM((n_features, hidden_width), BF16),
+            pltpu.SemaphoreType.DMA,
+        ],
+        compiler_params=pltpu.CompilerParams(vmem_limit_bytes=3 * 2**20),
         cost_estimate=pl.CostEstimate(flops=600 * 10**6, bytes_accessed=4 * 10**6, transcendentals=nodes * hidden_width),
         name="layer",
-    )(recv, adj, ww, bias.reshape(1, hidden_width), cotangent, lax.axis_index("core").reshape(1))
+    )(recv, adj, pltpu.with_memory_space_constraint(w_in, pltpu.MemorySpace.HBM), bias.reshape(1, hidden_width), cotangent, lax.axis_index("core").reshape(1))
 
     other = lax.ppermute(other, "core", [(0, 1), (1, 0)])
-    hidden, other = lax.optimization_barrier((hidden.astype(BF16), other))
     pair = (mine + other).astype(BF16)
     copies = jnp.broadcast_to(pair[:, None], (chips, row_size, width, hidden_width))
     copies = copies.reshape(chips * row_size, width, hidden_width)
     pieces = lax.all_to_all(copies, ("x", "rows"), split_axis=0, concat_axis=0, tiled=True)
-    return hidden, jnp.sum(pieces.astype(F32), axis=0)
+    return hidden.astype(BF16), jnp.sum(pieces.astype(F32), axis=0)
 
 
 def solution(mesh):

time: 48.4 us -> 50.6 us (1.045)
  blocking collectives: 18.1 us -> 0 us
  waiting for transfers between devices: 7.24 us -> 21.7 us
  starting transfers between devices: 11.2 us -> 16.1 us
  Pallas kernels: 4.72 us -> 5.75 us
    all_to_all x1 -> x0, blocking collectives: 18.1 us -> none  [body(): lax.all_to_all(copies, ('x', 'rows'), split_axis=0, concat_axis=0, tiled=...]
    all_to_all x0 -> x1, waiting for transfers between devices: none -> 12.7 us  [body(): lax.all_to_all(copies, ('x', 'rows'), split_axis=0, concat_axis=0, tiled=...]
    all_to_all x0 -> x1, starting transfers between devices: none -> 4.85 us  [body(): lax.all_to_all(copies, ('x', 'rows'), split_axis=0, concat_axis=0, tiled=...]
    pallas_call x1, Pallas kernels: 1.68 us -> 2.86 us  [body(): pl.pallas_call(layer_kernel, out_shape=(jax.ShapeDtypeStruct((nodes, hidd...]
    all_to_all x1, waiting for transfers between devices: 6.79 us -> 7.76 us  [body(): recv = lax.all_to_all(send, ALL, split_axis=0, concat_axis=0, tiled=True)]
    unnamed x14 -> x12, local copies, waits for them, and re-layouts: 4.56 us -> 3.67 us
    broadcast_in_dim x1, local copies, waits for them, and re-layouts: 0.04 us -> 0.83 us  [body(): jnp.broadcast_to(pair[:, None], (chips, row_size, width, hidden_width))]
    ppermute x1, waiting for transfers between devices: 0.45 us -> 1.24 us  [body(): other = lax.ppermute(other, 'core', [(0, 1), (1, 0)])]
  transfers between devices with their start and end apart: 2 -> 3, of which waited for: 2 -> 3; matrix products, arithmetic and copies ran while one was open for 2% -> 2% of each run, Pallas kernels for 4% -> 3%
where the time goes in v7:
time: 50.6 us; the launch traced here: 50.3 us
  waiting for transfers between devices  21.7 us (43%)
  starting transfers between devices  16.1 us (32%)
  Pallas kernels  5.75 us (11%)
  local copies, waits for them, and re-layouts  4.51 us (9%)
  other arithmetic  1.5 us (3%)
  between operations  0.72 us (1%)
    all_to_all x1, waiting for transfers between devices, body(): lax.all_to_all(copies, ('x', 'rows'), split_axis=0, concat_axis=0, tiled=...  12.7 us
    all_to_all x1, starting transfers between devices, body(): recv = lax.all_to_all(send, ALL, split_axis=0, concat_axis=0, tiled=True)  11.1 us
    all_to_all x1, waiting for transfers between devices, body(): recv = lax.all_to_all(send, ALL, split_axis=0, concat_axis=0, tiled=True)  7.76 us
    all_to_all x1, starting transfers between devices, body(): lax.all_to_all(copies, ('x', 'rows'), split_axis=0, concat_axis=0, tiled=...  4.85 us
    unnamed x12, local copies, waits for them, and re-layouts  3.67 us
    pallas_call x1, Pallas kernels, body(): pl.pallas_call(layer_kernel, out_shape=(jax.ShapeDtypeStruct((nodes, hidd...  2.86 us
    pallas_call x1, Pallas kernels, body(): pl.pallas_call(lambda *refs: adjacency_kernel(*refs, cycle=cycle), out_sh...  1.71 us
    ppermute x1, waiting for transfers between devices, body(): other = lax.ppermute(other, 'core', [(0, 1), (1, 0)])  1.24 us
  transfers between devices with their start and end apart: 3, of which 3 were waited for; matrix products, arithmetic and copies ran while one was open for 2% of the time, Pallas kernels for 3%

profile of v7, /device:TPU:0, one launch (start us, length us, event | category | flops | bytes accessed | tf_op | source)
XLA Modules:
  0.0 50.3 jit_solution(6921616536243026793)
XLA Ops:
  0.6 0.0 copy-start.2
  0.6 0.9 %copy-done.2 = bf16[16,128,48]{1,2,0:T(8,128)(2,1)S(1)} copy-done((bf16[16,128,48]{1,2,0:T(8,128)(2,1)S(1)}, bf16[16,128,48]{1,2,0:T(8,128)(2,1)}, u32[]{:S(2)}) %copy-start.2) | copy-done | bytes 196632
  1.6 1.2 %pieces.1 = bf16[128,4,384]{2,1,0:T(4,128)(2,1)} custom-call(s32[1]{0:T(128)} %bitcast.refs_0_, bf16[16,48,128]{2,1,0:T(8,128)(2,1)S(1)} %bitcast.8), custom_call_target="tpu_custom_call" | custom-call | tf_op jit(solution)/shard_map/pieces/pallas_call | solution.py:149
  2.8 0.0 copy-start.1
  2.8 11.1 %all-to-all-start = ((bf16[128,4,384]{2,1,0:T(4,128)(2,1)}), bf16[128,4,384]{2,1,0:T(4,128)(2,1)S(1)}, u32[]{:S(2)}, u32[]{:S(2)}) async-start(bf16[128,4,384]{2,1,0:T(4,128)(2,1)} %pieces.1), calls=%async_computation | async-start | bytes 786432 | tf_op jit(solution)/shard_map/all_to_all | solution.py:158
  13.9 0.0 copy-start.4
  13.9 0.0 copy-start
  13.9 1.4 %copy-done = bf16[6,8,128,128]{3,2,1,0:T(8,128)(2,1)S(1)} copy-done((bf16[6,8,128,128]{3,2,1,0:T(8,128)(2,1)S(1)}, bf16[6,8,128,128]{3,2,1,0:T(8,128)(2,1)}, u32[]{:S(2)}) %copy-start) | copy-done | bytes 1572888
  15.3 0.0 copy-start.3
  15.3 0.7 %copy-done.3 = s32[6,8]{1,0:T(8,128)S(1)} copy-done((s32[6,8]{1,0:T(8,128)S(1)}, s32[6,8]{1,0:T(8,128)}, u32[]{:S(2)}) %copy-start.3) | copy-done | bytes 216
  16.0 0.0 copy-start.5
  16.0 0.7 %copy-done.5 = s32[6]{0:T(128)S(1)} copy-done((s32[6]{0:T(128)S(1)}, s32[6]{0:T(128)}, u32[]{:S(2)}) %copy-start.5) | copy-done | bytes 48
  16.7 1.7 %adjacency.1.adj_ref = bf16[768,1280]{1,0:T(8,128)(2,1)S(1)} custom-call(s32[6,8]{1,0:T(8,128)S(1)} %copy-done.3, s32[6]{0:T(128)S(1)} %copy-done.5, s32[1]{0:T(128)} %bitcast.3.refs_2_, bf16[6,8,128,128]{3,2,1,0:T(8,128)(2,1)S(1)} %copy-done), custom_call_target="tpu_custom_call" | custom-call | flops 2000000 | bytes 4000000 | tf_op jit(solution)/shard_map/adjacency/pallas_call | solution.py:163
  18.4 7.8 %all-to-all-done = bf16[128,4,384]{2,1,0:T(4,128)(2,1)S(1)} async-done(((bf16[128,4,384]{2,1,0:T(4,128)(2,1)}), bf16[128,4,384]{2,1,0:T(4,128)(2,1)S(1)}, u32[]{:S(2)}, u32[]{:S(2)}) %all-to-all-start) | async-done | bytes 393248 | tf_op jit(solution)/shard_map/all_to_all | solution.py:158
  26.2 0.0 copy-done.1
  26.2 0.0 copy-done.4
  26.2 2.9 %layer.1 = (f32[768,256]{1,0:T(8,128)S(1)}, f32[4,16,256]{2,1,0:T(8,128)S(1)}, f32[4,16,256]{2,1,0:T(8,128)S(1)}) custom-call(bf16[8,16,4,384]{3,2,1,0:T(4,128)(2,1)S(1)} %bitcast.7, bf16[768,1280]{1,0:T(8,128)(2,1)S(1)} %adjacency.1.adj_ref, bf16[128,256]{1,0:T(8,128)(2,1)} %w_hbm.1, f32[1,256]{1,0:T(1,128)S(1)} %bitcast.9, bf16[768,256]{1,0:T(8,128)(2,1)S(1)} %copy-done.1, ...), custom_call_target="tpu_custom_call" | custom-call | flops 600000000 | bytes 4000000 | tf_op jit(solution)/shard_map/layer/pallas_call | solution.py:174
  29.0 0.1 collective-permute-start
  29.1 1.2 %collective-permute-done = f32[4,16,256]{2,1,0:T(8,128)S(1)} collective-permute-done((f32[4,16,256]{2,1,0:T(8,128)S(1)}, f32[4,16,256]{2,1,0:T(8,128)S(1)}, u32[]{:S(2)}, u32[]{:S(2)}) %collective-permute-start) | collective-permute-done | bytes 65568 | tf_op jit(solution)/shard_map/ppermute | solution.py:189
  30.4 0.8 %broadcast_in_dim.2 = bf16[4,16,16,256]{3,2,1,0:T(8,128)(2,1)} broadcast(bf16[4,16,256]{2,1,0:T(8,128)(2,1)S(1)} %add_convert_fusion), dimensions={0,2,3} | broadcast | bytes 557056 | tf_op jit(solution)/shard_map/broadcast_in_dim | solution.py:191
  31.2 4.9 %all-to-all-start.1 = ((bf16[64,16,256]{2,1,0:T(8,128)(2,1)}), bf16[64,16,256]{2,1,0:T(8,128)(2,1)S(1)}, u32[]{:S(2)}, u32[]{:S(2)}) async-start(bf16[64,16,256]{2,1,0:T(8,128)(2,1)} %bitcast.6), calls=%async_computation.1 | async-start | bytes 1048576 | tf_op jit(solution)/shard_map/all_to_all | solution.py:193
  36.1 0.8 %convert_element_type.9 = bf16[768,256]{1,0:T(8,128)(2,1)} convert(f32[768,256]{1,0:T(8,128)S(1)} %get-tuple-element.5) | non-fusion elementwise | flops 196608 | bytes 1179648 | tf_op jit(solution)/shard_map/convert_element_type | solution.py:194
  36.9 12.7 %all-to-all-done.1 = bf16[64,16,256]{2,1,0:T(8,128)(2,1)S(1)} async-done(((bf16[64,16,256]{2,1,0:T(8,128)(2,1)}), bf16[64,16,256]{2,1,0:T(8,128)(2,1)S(1)}, u32[]{:S(2)}, u32[]{:S(2)}) %all-to-all-start.1) | async-done | bytes 524320 | tf_op jit(solution)/shard_map/all_to_all | solution.py:193
  49.6 0.7 %convert_reduce_fusion = f32[16,256]{1,0:T(8,128)} fusion(bf16[64,16,256]{2,1,0:T(8,128)(2,1)S(1)} %all-to-all-done.1), kind=kLoop, calls=%fused_computation | loop fusion | flops 520192 | bytes 540672 | tf_op jit(solution)/shard_map/reduce_sum | solution.py:194
  (1 shorter events, 0.0 us)
Async XLA Ops:
  0.6 0.9 %copy-start.2 = (bf16[16,128,48]{1,2,0:T(8,128)(2,1)S(1)}, bf16[16,128,48]{1,2,0:T(8,128)(2,1)}, u32[]{:S(2)}) copy-start(bf16[16,128,48]{1,2,0:T(8,128)(2,1)} %param.7) | copy-start | bytes 589828
  2.8 23.4 %copy-start.1 = (bf16[768,256]{1,0:T(8,128)(2,1)S(1)}, bf16[768,256]{1,0:T(8,128)(2,1)}, u32[]{:S(2)}) copy-start(bf16[768,256]{1,0:T(8,128)(2,1)} %cot_ref.1) | copy-start | bytes 1179652
  2.8 23.4 %all-to-all-start = ((bf16[128,4,384]{2,1,0:T(4,128)(2,1)}), bf16[128,4,384]{2,1,0:T(4,128)(2,1)S(1)}, u32[]{:S(2)}, u32[]{:S(2)}) async-start(bf16[128,4,384]{2,1,0:T(4,128)(2,1)} %pieces.1), calls=%async_computation | async-start | bytes 786432 | tf_op jit(solution)/shard_map/all_to_all | solution.py:158
  13.9 12.3 %copy-start.4 = (f32[256]{0:T(256)S(1)}, f32[256]{0:T(256)}, u32[]{:S(2)}) copy-start(f32[256]{0:T(256)} %param.9) | copy-start | bytes 3076
  13.9 1.4 %copy-start = (bf16[6,8,128,128]{3,2,1,0:T(8,128)(2,1)S(1)}, bf16[6,8,128,128]{3,2,1,0:T(8,128)(2,1)}, u32[]{:S(2)}) copy-start(bf16[6,8,128,128]{3,2,1,0:T(8,128)(2,1)} %refs_3_.1) | copy-start | bytes 4718596
  15.3 0.7 %copy-start.3 = (s32[6,8]{1,0:T(8,128)S(1)}, s32[6,8]{1,0:T(8,128)}, u32[]{:S(2)}) copy-start(s32[6,8]{1,0:T(8,128)} %refs_0_.1) | copy-start | bytes 580
  16.0 0.7 %copy-start.5 = (s32[6]{0:T(128)S(1)}, s32[6]{0:T(128)}, u32[]{:S(2)}) copy-start(s32[6]{0:T(128)} %refs_1_.1) | copy-start | bytes 76
  29.0 1.3 %collective-permute-start = (f32[4,16,256]{2,1,0:T(8,128)S(1)}, f32[4,16,256]{2,1,0:T(8,128)S(1)}, u32[]{:S(2)}, u32[]{:S(2)}) collective-permute-start(f32[4,16,256]{2,1,0:T(8,128)S(1)} %get-tuple-element.7), channel_id=1, source_target_pairs={{0,16},{16,0},{1,17},{17,1},{2,18},{18,2},{3,19},{19,3},{4,20},{20... | collective-permute-start | bytes 196616 | tf_op jit(solution)/shard_map/ppermute | solution.py:189
  31.2 18.3 %all-to-all-start.1 = ((bf16[64,16,256]{2,1,0:T(8,128)(2,1)}), bf16[64,16,256]{2,1,0:T(8,128)(2,1)S(1)}, u32[]{:S(2)}, u32[]{:S(2)}) async-start(bf16[64,16,256]{2,1,0:T(8,128)(2,1)} %bitcast.6), calls=%async_computation.1 | async-start | bytes 1048576 | tf_op jit(solution)/shard_map/all_to_all | solution.py:193

commit v8 on v6

--- a/solution.py
+++ b/solution.py
@@ -48,22 +48,15 @@
                 adj_ref[at] = adj_ref[at] + tiles_ref[b, k]
 
 
-def send_kernel(step_ref, x_hbm, out_hbm, x_ref, rows_ref, out_ref, load_sem, store_sem, *, ring):
+def send_kernel(step_ref, x_ref, out_hbm, rows_ref, out_ref, store_sem, *, ring):
     width, part, owners = x_ref.shape
     quarter = width // PARTS
     third = LANES - 2 * part
-    loads = []
-    for n in range(COPIES):
-        at = pl.ds(n * (width // COPIES), width // COPIES)
-        loads.append(pltpu.make_async_copy(x_hbm.at[at], x_ref.at[at], load_sem.at[n]))
-        loads[n].start()
     i = lax.broadcasted_iota(jnp.int32, (owners, owners), 0)
     k = lax.broadcasted_iota(jnp.int32, (owners, owners), 1)
     beside = (i // ring) * ring + lax.rem(lax.rem(i, ring) + step_ref[0] + ring, ring)
     pick = jnp.concatenate([jnp.where(k == i, 1.0, 0.0), jnp.where(k == beside, 1.0, 0.0)], axis=1).astype(BF16)
     none = jnp.zeros((part, owners), BF16)
-    for load in loads:
-        load.wait()
 
     def both(c):
         x = x_ref[c]
@@ -161,23 +154,20 @@
     vmem = pl.BlockSpec(memory_space=pltpu.VMEM)
     smem = pl.BlockSpec(memory_space=pltpu.SMEM)
     step = jnp.where(row_id * 2 < row_size, 1, -1).reshape(1).astype(jnp.int32)
-    hbm = pl.BlockSpec(memory_space=pltpu.MemorySpace.HBM)
     sent = (owners, width // PARTS, (PARTS - 1) * LANES)
     send = pl.pallas_call(
         lambda *refs: send_kernel(*refs, ring=row_size),
         out_shape=jax.ShapeDtypeStruct(sent, BF16),
-        in_specs=[smem, hbm],
-        out_specs=hbm,
+        in_specs=[smem, vmem],
+        out_specs=pl.BlockSpec(memory_space=pltpu.MemorySpace.HBM),
         scratch_shapes=[
-            pltpu.VMEM((width, part, owners), BF16),
             pltpu.VMEM((owners * (width - width // PARTS), LANES), F32),
             pltpu.VMEM(sent, BF16),
-            pltpu.SemaphoreType.DMA((COPIES,)),
             pltpu.SemaphoreType.DMA((COPIES,)),
         ],
         compiler_params=pltpu.CompilerParams(vmem_limit_bytes=4 * 2**20),
         name="pieces",
-    )(step, pltpu.with_memory_space_constraint(features.transpose(0, 2, 1), pltpu.MemorySpace.HBM))
+    )(step, features.transpose(0, 2, 1))
     recv = lax.all_to_all(send, ALL, split_axis=0, concat_axis=0, tiled=True)
     recv = recv.reshape(feat_size, row_size, width // PARTS, (PARTS - 1) * LANES)
 

time: 48.4 us -> 48.4 us (level)
  Pallas kernels: 5.72 us -> 4.48 us
  local copies, waits for them, and re-layouts: 3.63 us -> 4.59 us
    pallas_call x1, Pallas kernels: 2.17 us -> 1.16 us  [body(): pl.pallas_call(lambda *refs: send_kernel(*refs, ring=row_size), out_shape...]
    unnamed x12 -> x14, local copies, waits for them, and re-layouts: 3.59 us -> 4.56 us
  transfers between devices with their start and end apart: 2 -> 2, of which waited for: 2 -> 2; matrix products, arithmetic and copies ran while one was open for 2% -> 2% of each run, Pallas kernels for 4% -> 3%
where the time goes in v8:
time: 48.4 us; the launch traced here: 48.1 us
  blocking collectives  18.1 us (37%)
  starting transfers between devices  11.2 us (23%)
  waiting for transfers between devices  7.45 us (15%)
  local copies, waits for them, and re-layouts  4.59 us (9%)
  Pallas kernels  4.48 us (9%)
  other arithmetic  1.5 us (3%)
  between operations  0.73 us (2%)
    all_to_all x1, blocking collectives, body(): lax.all_to_all(copies, ('x', 'rows'), split_axis=0, concat_axis=0, tiled=...  18.1 us
    all_to_all x1, starting transfers between devices, body(): recv = lax.all_to_all(send, ALL, split_axis=0, concat_axis=0, tiled=True)  11.1 us
    all_to_all x1, waiting for transfers between devices, body(): recv = lax.all_to_all(send, ALL, split_axis=0, concat_axis=0, tiled=True)  6.99 us
    unnamed x14, local copies, waits for them, and re-layouts  4.56 us
    pallas_call x1, Pallas kernels, body(): pl.pallas_call(layer_kernel, out_shape=(jax.ShapeDtypeStruct((nodes, hidd...  1.68 us
    pallas_call x1, Pallas kernels, body(): pl.pallas_call(lambda *refs: adjacency_kernel(*refs, cycle=cycle, slices=...  1.64 us
    pallas_call x1, Pallas kernels, body(): pl.pallas_call(lambda *refs: send_kernel(*refs, ring=row_size), out_shape...  1.16 us
  transfers between devices with their start and end apart: 2, of which 2 were waited for; matrix products, arithmetic and copies ran while one was open for 2% of the time, Pallas kernels for 3%

profile of v8, /device:TPU:0, one launch (start us, length us, event | category | flops | bytes accessed | tf_op | source)
XLA Modules:
  0.0 48.1 jit_solution(2142257224766232571)
XLA Ops:
  0.6 0.0 copy-start.1
  0.6 0.0 copy-start.2
  0.7 1.0 %copy-done.2 = bf16[16,128,48]{1,2,0:T(8,128)(2,1)S(1)} copy-done((bf16[16,128,48]{1,2,0:T(8,128)(2,1)S(1)}, bf16[16,128,48]{1,2,0:T(8,128)(2,1)}, u32[]{:S(2)}) %copy-start.2) | copy-done | bytes 196632
  1.6 0.0 copy-start.5
  1.6 1.2 %pieces.1 = bf16[128,4,384]{2,1,0:T(4,128)(2,1)} custom-call(s32[1]{0:T(128)} %bitcast.refs_0_, bf16[16,48,128]{2,1,0:T(8,128)(2,1)S(1)} %bitcast.8), custom_call_target="tpu_custom_call" | custom-call | tf_op jit(solution)/shard_map/pieces/pallas_call | solution.py:158
  2.8 11.1 %all-to-all-start = ((bf16[128,4,384]{2,1,0:T(4,128)(2,1)}), bf16[128,4,384]{2,1,0:T(4,128)(2,1)S(1)}, u32[]{:S(2)}, u32[]{:S(2)}) async-start(bf16[128,4,384]{2,1,0:T(4,128)(2,1)} %pieces.1), calls=%async_computation | async-start | bytes 786432 | tf_op jit(solution)/shard_map/all_to_all | solution.py:171
  14.0 0.0 copy-start
  14.0 1.4 %copy-done = bf16[6,8,128,128]{3,2,1,0:T(8,128)(2,1)S(1)} copy-done((bf16[6,8,128,128]{3,2,1,0:T(8,128)(2,1)S(1)}, bf16[6,8,128,128]{3,2,1,0:T(8,128)(2,1)}, u32[]{:S(2)}) %copy-start) | copy-done | bytes 1572888
  15.4 0.0 copy-start.3
  15.4 0.8 %copy-done.3 = bf16[128,256]{1,0:T(8,128)(2,1)S(1)} copy-done((bf16[128,256]{1,0:T(8,128)(2,1)S(1)}, bf16[128,256]{1,0:T(8,128)(2,1)}, u32[]{:S(2)}) %copy-start.3) | copy-done | bytes 65560
  16.2 0.0 copy-start.4
  16.2 0.7 %copy-done.4 = s32[6,8]{1,0:T(8,128)S(1)} copy-done((s32[6,8]{1,0:T(8,128)S(1)}, s32[6,8]{1,0:T(8,128)}, u32[]{:S(2)}) %copy-start.4) | copy-done | bytes 216
  16.9 0.0 copy-start.6
  16.9 0.7 %copy-done.6 = s32[6]{0:T(128)S(1)} copy-done((s32[6]{0:T(128)S(1)}, s32[6]{0:T(128)}, u32[]{:S(2)}) %copy-start.6) | copy-done | bytes 48
  17.6 1.6 %adjacency.1 = (bf16[768,1280]{1,0:T(8,128)(2,1)S(1)}, bf16[256,256]{1,0:T(8,128)(2,1)S(1)}) custom-call(s32[6,8]{1,0:T(8,128)S(1)} %copy-done.4, s32[6]{0:T(128)S(1)} %copy-done.6, s32[1]{0:T(128)} %bitcast.3.refs_2_, bf16[6,8,128,128]{3,2,1,0:T(8,128)(2,1)S(1)} %copy-done, bf16[128,256]{1,0:T(8,128)(2,1)S(1)} %copy-done.3), custom_call_target="tpu_custom_call" | custom-call | flops 2000000 | bytes 4000000 | tf_op jit(solution)/shard_map/adjacency/pallas_call | solution.py:176
  19.2 7.0 %all-to-all-done = bf16[128,4,384]{2,1,0:T(4,128)(2,1)S(1)} async-done(((bf16[128,4,384]{2,1,0:T(4,128)(2,1)}), bf16[128,4,384]{2,1,0:T(4,128)(2,1)S(1)}, u32[]{:S(2)}, u32[]{:S(2)}) %all-to-all-start) | async-done | bytes 393248 | tf_op jit(solution)/shard_map/all_to_all | solution.py:171
  26.2 0.0 copy-done.1
  26.2 0.0 copy-done.5
  26.2 1.7 %layer.1 = (f32[768,256]{1,0:T(8,128)S(1)}, f32[4,16,256]{2,1,0:T(8,128)S(1)}, f32[4,16,256]{2,1,0:T(8,128)S(1)}) custom-call(bf16[8,16,4,384]{3,2,1,0:T(4,128)(2,1)S(1)} %bitcast.7, bf16[768,1280]{1,0:T(8,128)(2,1)S(1)} %get-tuple-element.9.adj_ref, bf16[256,256]{1,0:T(8,128)(2,1)S(1)} %get-tuple-element.10.ww_ref, f32[1,256]{1,0:T(1,128)S(1)} %bitcast.9, ...), custom_call_target="tpu_custom_call" | custom-call | flops 600000000 | bytes 4000000 | tf_op jit(solution)/shard_map/layer/pallas_call | solution.py:190
  27.9 0.1 collective-permute-start
  28.0 0.8 %convert_element_type.9 = bf16[768,256]{1,0:T(8,128)(2,1)} convert(f32[768,256]{1,0:T(8,128)S(1)} %get-tuple-element.11) | non-fusion elementwise | flops 196608 | bytes 1179648 | tf_op jit(solution)/shard_map/convert_element_type | solution.py:202
  28.8 0.5 collective-permute-done
  29.3 18.1 %all_to_all.10 = bf16[64,16,256]{2,1,0:T(8,128)(2,1)S(1)} all-to-all(bf16[64,16,256]{2,1,0:T(8,128)(2,1)S(1)} %bitcast.10), channel_id=1, replica_groups=mesh['x'=4,'core'=2,'rows'=16] {'x','rows'}, dimensions={0} | all-to-all | bytes 1048576 | tf_op jit(solution)/shard_map/all_to_all | solution.py:206
  47.4 0.7 %convert_reduce_fusion = f32[16,256]{1,0:T(8,128)} fusion(bf16[64,16,256]{2,1,0:T(8,128)(2,1)S(1)} %all_to_all.10), kind=kLoop, calls=%fused_computation | loop fusion | flops 520192 | bytes 540672 | tf_op jit(solution)/shard_map/reduce_sum | solution.py:207
  (2 shorter events, 0.0 us)
Async XLA Ops:
  0.6 25.6 %copy-start.1 = (bf16[768,256]{1,0:T(8,128)(2,1)S(1)}, bf16[768,256]{1,0:T(8,128)(2,1)}, u32[]{:S(2)}) copy-start(bf16[768,256]{1,0:T(8,128)(2,1)} %cot_ref.1) | copy-start | bytes 1179652
  0.6 1.0 %copy-start.2 = (bf16[16,128,48]{1,2,0:T(8,128)(2,1)S(1)}, bf16[16,128,48]{1,2,0:T(8,128)(2,1)}, u32[]{:S(2)}) copy-start(bf16[16,128,48]{1,2,0:T(8,128)(2,1)} %param.7) | copy-start | bytes 589828
  1.6 24.6 %copy-start.5 = (f32[256]{0:T(256)S(1)}, f32[256]{0:T(256)}, u32[]{:S(2)}) copy-start(f32[256]{0:T(256)} %param.9) | copy-start | bytes 3076
  2.8 23.4 %all-to-all-start = ((bf16[128,4,384]{2,1,0:T(4,128)(2,1)}), bf16[128,4,384]{2,1,0:T(4,128)(2,1)S(1)}, u32[]{:S(2)}, u32[]{:S(2)}) async-start(bf16[128,4,384]{2,1,0:T(4,128)(2,1)} %pieces.1), calls=%async_computation | async-start | bytes 786432 | tf_op jit(solution)/shard_map/all_to_all | solution.py:171
  14.0 1.4 %copy-start = (bf16[6,8,128,128]{3,2,1,0:T(8,128)(2,1)S(1)}, bf16[6,8,128,128]{3,2,1,0:T(8,128)(2,1)}, u32[]{:S(2)}) copy-start(bf16[6,8,128,128]{3,2,1,0:T(8,128)(2,1)} %refs_3_.1) | copy-start | bytes 4718596
  15.4 0.8 %copy-start.3 = (bf16[128,256]{1,0:T(8,128)(2,1)S(1)}, bf16[128,256]{1,0:T(8,128)(2,1)}, u32[]{:S(2)}) copy-start(bf16[128,256]{1,0:T(8,128)(2,1)} %refs_4_.1) | copy-start | bytes 196612
  16.2 0.7 %copy-start.4 = (s32[6,8]{1,0:T(8,128)S(1)}, s32[6,8]{1,0:T(8,128)}, u32[]{:S(2)}) copy-start(s32[6,8]{1,0:T(8,128)} %refs_0_.1) | copy-start | bytes 580
  16.9 0.7 %copy-start.6 = (s32[6]{0:T(128)S(1)}, s32[6]{0:T(128)}, u32[]{:S(2)}) copy-start(s32[6]{0:T(128)} %refs_1_.1) | copy-start | bytes 76
  27.9 1.3 %collective-permute-start = (f32[4,16,256]{2,1,0:T(8,128)S(1)}, f32[4,16,256]{2,1,0:T(8,128)S(1)}, u32[]{:S(2)}, u32[]{:S(2)}) collective-permute-start(f32[4,16,256]{2,1,0:T(8,128)S(1)} %get-tuple-element.12), channel_id=1, source_target_pairs={{0,16},{16,0},{1,17},{17,1},{2,18},{18,2},{3,19},{19,3},{4,20},{20... | collective-permute-start | bytes 196616 | tf_op jit(solution)/shard_map/ppermute | solution.py:201

commit v9 on v5

--- a/solution.py
+++ b/solution.py
@@ -187,9 +187,9 @@
     other = lax.ppermute(other, "core", [(0, 1), (1, 0)])
     hidden, other = lax.optimization_barrier((hidden.astype(BF16), other))
     pair = (mine + other).astype(BF16)
-    copies = jnp.broadcast_to(pair[:, None], (chips, row_size, width, hidden_width))
+    copies = jnp.broadcast_to(pair[None], (row_size, chips, width, hidden_width))
     copies = copies.reshape(chips * row_size, width, hidden_width)
-    pieces = lax.all_to_all(copies, ("x", "rows"), split_axis=0, concat_axis=0, tiled=True)
+    pieces = lax.all_to_all(copies, ("rows", "x"), split_axis=0, concat_axis=0, tiled=True)
     return hidden, jnp.sum(pieces.astype(F32), axis=0)
 
 

time: 48.4 us -> 48.7 us (level)
  no operation moved by 1% of the time
where the time goes in v9:
time: 48.7 us; the launch traced here: 48.4 us
  blocking collectives  18.3 us (38%)
  starting transfers between devices  11.2 us (23%)
  waiting for transfers between devices  7.21 us (15%)
  Pallas kernels  4.75 us (10%)
  local copies, waits for them, and re-layouts  4.6 us (9%)
  other arithmetic  1.5 us (3%)
  between operations  0.72 us (1%)
    all_to_all x1, blocking collectives, body(): lax.all_to_all(copies, ('rows', 'x'), split_axis=0, concat_axis=0, tiled=...  18.3 us
    all_to_all x1, starting transfers between devices, body(): recv = lax.all_to_all(send, ALL, split_axis=0, concat_axis=0, tiled=True)  11.1 us
    all_to_all x1, waiting for transfers between devices, body(): recv = lax.all_to_all(send, ALL, split_axis=0, concat_axis=0, tiled=True)  6.75 us
    unnamed x14, local copies, waits for them, and re-layouts  4.56 us
    pallas_call x1, Pallas kernels, body(): pl.pallas_call(lambda *refs: adjacency_kernel(*refs, cycle=cycle, slices=...  1.88 us
    pallas_call x1, Pallas kernels, body(): pl.pallas_call(layer_kernel, out_shape=(jax.ShapeDtypeStruct((nodes, hidd...  1.68 us
    pallas_call x1, Pallas kernels, body(): pl.pallas_call(lambda *refs: send_kernel(*refs, ring=row_size), out_shape...  1.19 us
  transfers between devices with their start and end apart: 2, of which 2 were waited for; matrix products, arithmetic and copies ran while one was open for 2% of the time, Pallas kernels for 4%

profile of v9, /device:TPU:0, one launch (start us, length us, event | category | flops | bytes accessed | tf_op | source)
XLA Modules:
  0.0 48.4 jit_solution(8254451832913809542)
XLA Ops:
  0.6 0.0 copy-start.1
  0.6 0.0 copy-start.2
  0.7 1.0 %copy-done.2 = bf16[16,128,48]{1,2,0:T(8,128)(2,1)S(1)} copy-done((bf16[16,128,48]{1,2,0:T(8,128)(2,1)S(1)}, bf16[16,128,48]{1,2,0:T(8,128)(2,1)}, u32[]{:S(2)}) %copy-start.2) | copy-done | bytes 196632
  1.6 0.0 copy-start.5
  1.6 1.2 %pieces.1 = bf16[128,4,384]{2,1,0:T(4,128)(2,1)} custom-call(s32[1]{0:T(128)} %bitcast.refs_0_, bf16[16,48,128]{2,1,0:T(8,128)(2,1)S(1)} %bitcast.8), custom_call_target="tpu_custom_call" | custom-call | tf_op jit(solution)/shard_map/pieces/pallas_call | solution.py:148
  2.8 11.1 %all-to-all-start = ((bf16[128,4,384]{2,1,0:T(4,128)(2,1)}), bf16[128,4,384]{2,1,0:T(4,128)(2,1)S(1)}, u32[]{:S(2)}, u32[]{:S(2)}) async-start(bf16[128,4,384]{2,1,0:T(4,128)(2,1)} %pieces.1), calls=%async_computation | async-start | bytes 786432 | tf_op jit(solution)/shard_map/all_to_all | solution.py:157
  14.0 0.0 copy-start
  14.0 1.4 %copy-done = bf16[6,8,128,128]{3,2,1,0:T(8,128)(2,1)S(1)} copy-done((bf16[6,8,128,128]{3,2,1,0:T(8,128)(2,1)S(1)}, bf16[6,8,128,128]{3,2,1,0:T(8,128)(2,1)}, u32[]{:S(2)}) %copy-start) | copy-done | bytes 1572888
  15.4 0.0 copy-start.3
  15.4 0.8 %copy-done.3 = bf16[128,256]{1,0:T(8,128)(2,1)S(1)} copy-done((bf16[128,256]{1,0:T(8,128)(2,1)S(1)}, bf16[128,256]{1,0:T(8,128)(2,1)}, u32[]{:S(2)}) %copy-start.3) | copy-done | bytes 65560
  16.2 0.0 copy-start.4
  16.2 0.7 %copy-done.4 = s32[6,8]{1,0:T(8,128)S(1)} copy-done((s32[6,8]{1,0:T(8,128)S(1)}, s32[6,8]{1,0:T(8,128)}, u32[]{:S(2)}) %copy-start.4) | copy-done | bytes 216
  16.9 0.0 copy-start.6
  16.9 0.7 %copy-done.6 = s32[6]{0:T(128)S(1)} copy-done((s32[6]{0:T(128)S(1)}, s32[6]{0:T(128)}, u32[]{:S(2)}) %copy-start.6) | copy-done | bytes 48
  17.6 1.9 %adjacency.1 = (bf16[768,1280]{1,0:T(8,128)(2,1)S(1)}, bf16[256,256]{1,0:T(8,128)(2,1)S(1)}) custom-call(s32[6,8]{1,0:T(8,128)S(1)} %copy-done.4, s32[6]{0:T(128)S(1)} %copy-done.6, s32[1]{0:T(128)} %bitcast.3.refs_2_, bf16[6,8,128,128]{3,2,1,0:T(8,128)(2,1)S(1)} %copy-done, bf16[128,256]{1,0:T(8,128)(2,1)S(1)} %copy-done.3), custom_call_target="tpu_custom_call" | custom-call | flops 2000000 | bytes 4000000 | tf_op jit(solution)/shard_map/adjacency/pallas_call | solution.py:162
  19.5 6.8 %all-to-all-done = bf16[128,4,384]{2,1,0:T(4,128)(2,1)S(1)} async-done(((bf16[128,4,384]{2,1,0:T(4,128)(2,1)}), bf16[128,4,384]{2,1,0:T(4,128)(2,1)S(1)}, u32[]{:S(2)}, u32[]{:S(2)}) %all-to-all-start) | async-done | bytes 393248 | tf_op jit(solution)/shard_map/all_to_all | solution.py:157
  26.2 0.0 copy-done.1
  26.2 0.0 copy-done.5
  26.2 1.7 %layer.1 = (f32[768,256]{1,0:T(8,128)S(1)}, f32[4,16,256]{2,1,0:T(8,128)S(1)}, f32[4,16,256]{2,1,0:T(8,128)S(1)}) custom-call(bf16[8,16,4,384]{3,2,1,0:T(4,128)(2,1)S(1)} %bitcast.7, bf16[768,1280]{1,0:T(8,128)(2,1)S(1)} %get-tuple-element.9.adj_ref, bf16[256,256]{1,0:T(8,128)(2,1)S(1)} %get-tuple-element.10.ww_ref, f32[1,256]{1,0:T(1,128)S(1)} %bitcast.9, ...), custom_call_target="tpu_custom_call" | custom-call | flops 600000000 | bytes 4000000 | tf_op jit(solution)/shard_map/layer/pallas_call | solution.py:176
  27.9 0.1 collective-permute-start
  28.0 0.8 %convert_element_type.9 = bf16[768,256]{1,0:T(8,128)(2,1)} convert(f32[768,256]{1,0:T(8,128)S(1)} %get-tuple-element.11) | non-fusion elementwise | flops 196608 | bytes 1179648 | tf_op jit(solution)/shard_map/convert_element_type | solution.py:188
  28.8 0.5 collective-permute-done
  29.3 18.3 %all_to_all.10 = bf16[64,16,256]{2,1,0:T(8,128)(2,1)S(1)} all-to-all(bf16[64,16,256]{2,1,0:T(8,128)(2,1)S(1)} %bitcast.10), channel_id=1, replica_groups=mesh['x'=4,'core'=2,'rows'=16] {'rows','x'}, dimensions={0} | all-to-all | bytes 1048576 | tf_op jit(solution)/shard_map/all_to_all | solution.py:192
  47.6 0.7 %convert_reduce_fusion = f32[16,256]{1,0:T(8,128)} fusion(bf16[64,16,256]{2,1,0:T(8,128)(2,1)S(1)} %all_to_all.10), kind=kLoop, calls=%fused_computation | loop fusion | flops 520192 | bytes 540672 | tf_op jit(solution)/shard_map/reduce_sum | solution.py:193
  (2 shorter events, 0.1 us)
Async XLA Ops:
  0.6 25.6 %copy-start.1 = (bf16[768,256]{1,0:T(8,128)(2,1)S(1)}, bf16[768,256]{1,0:T(8,128)(2,1)}, u32[]{:S(2)}) copy-start(bf16[768,256]{1,0:T(8,128)(2,1)} %cot_ref.1) | copy-start | bytes 1179652
  0.6 1.0 %copy-start.2 = (bf16[16,128,48]{1,2,0:T(8,128)(2,1)S(1)}, bf16[16,128,48]{1,2,0:T(8,128)(2,1)}, u32[]{:S(2)}) copy-start(bf16[16,128,48]{1,2,0:T(8,128)(2,1)} %param.7) | copy-start | bytes 589828
  1.6 24.6 %copy-start.5 = (f32[256]{0:T(256)S(1)}, f32[256]{0:T(256)}, u32[]{:S(2)}) copy-start(f32[256]{0:T(256)} %param.9) | copy-start | bytes 3076
  2.8 23.4 %all-to-all-start = ((bf16[128,4,384]{2,1,0:T(4,128)(2,1)}), bf16[128,4,384]{2,1,0:T(4,128)(2,1)S(1)}, u32[]{:S(2)}, u32[]{:S(2)}) async-start(bf16[128,4,384]{2,1,0:T(4,128)(2,1)} %pieces.1), calls=%async_computation | async-start | bytes 786432 | tf_op jit(solution)/shard_map/all_to_all | solution.py:157
  14.0 1.4 %copy-start = (bf16[6,8,128,128]{3,2,1,0:T(8,128)(2,1)S(1)}, bf16[6,8,128,128]{3,2,1,0:T(8,128)(2,1)}, u32[]{:S(2)}) copy-start(bf16[6,8,128,128]{3,2,1,0:T(8,128)(2,1)} %refs_3_.1) | copy-start | bytes 4718596
  15.4 0.8 %copy-start.3 = (bf16[128,256]{1,0:T(8,128)(2,1)S(1)}, bf16[128,256]{1,0:T(8,128)(2,1)}, u32[]{:S(2)}) copy-start(bf16[128,256]{1,0:T(8,128)(2,1)} %refs_4_.1) | copy-start | bytes 196612
  16.2 0.7 %copy-start.4 = (s32[6,8]{1,0:T(8,128)S(1)}, s32[6,8]{1,0:T(8,128)}, u32[]{:S(2)}) copy-start(s32[6,8]{1,0:T(8,128)} %refs_0_.1) | copy-start | bytes 580
  16.9 0.7 %copy-start.6 = (s32[6]{0:T(128)S(1)}, s32[6]{0:T(128)}, u32[]{:S(2)}) copy-start(s32[6]{0:T(128)} %refs_1_.1) | copy-start | bytes 76
  27.9 1.3 %collective-permute-start = (f32[4,16,256]{2,1,0:T(8,128)S(1)}, f32[4,16,256]{2,1,0:T(8,128)S(1)}, u32[]{:S(2)}, u32[]{:S(2)}) collective-permute-start(f32[4,16,256]{2,1,0:T(8,128)S(1)} %get-tuple-element.12), channel_id=1, source_target_pairs={{0,16},{16,0},{1,17},{17,1},{2,18},{18,2},{3,19},{19,3},{4,20},{20... | collective-permute-start | bytes 196616 | tf_op jit(solution)/shard_map/ppermute | solution.py:187
